TPU v7x, 512 devices: a whole 4x4x16 slice. The times are simulated.
512 devices in a mesh: group: 4 (over x_hi, core), slab: 128 (over z, y, x_lo).
Axes of the slice: x: 4 (x_hi: 2, x_lo: 2; x = x_hi * 2 + x_lo), y: 4, z: 16, core: 2. Of those that a mesh axis runs over, the one named last changes fastest.
Arguments:
- populations: float32 [19, 2048, 16, 128], P(None, ('group', 'slab')), may hold values from 0 to 1, as said below
- cell_kind: int32 [2048, 16, 128], P(('group', 'slab')), may hold values from 0 to 2, as said below
- snapshot_order: int32 [4], replicated, may hold values from 0 to 3, each once
- sample_phase: int32 [3], replicated, may hold values from 0 to 3
- slab_map: int32 [384], replicated, may hold values from 0 to 383, each once
- weighted_modes: float32 [589824, 252], P(('group', 'slab')), may hold values from -0.6 to 0.6
Outputs:
- lattice: float32 [19, 2048, 16, 128], P(None, ('group', 'slab'))
- basis_rows: float32 [589824, 256], P(('group', 'slab'))
Inputs may be any that keep to these rules, and one draw needn't show every extreme that they name: `populations`: each population lies between 0.4 and 1.6 times the weight of its direction. `cell_kind`: 0 marks a fluid cell, 1 a wall cell, 2 an inlet cell. `snapshot_order`: a permutation of the steps. `slab_map`: a permutation of the row blocks.
All inputs are finite; a program needn't handle non-finite values.
Results may differ from a plain program's by a relative error of at most 0.0003.
Values sent between devices are 32-bit elements; how exact they have to be, the bound alone decides.
A program may use at most 64 MiB of HBM per device.

v0:
```python
import math

import jax
import jax.numpy as jnp
from jax import lax
from jax.sharding import PartitionSpec as P

STEPS = 4
SUB = 4


lattice_dirs = [
    (0, 0, 0),
    (1, 0, 0),
    (-1, 0, 0),
    (0, 1, 0),
    (0, -1, 0),
    (0, 0, 1),
    (0, 0, -1),
    (1, 1, 0),
    (-1, -1, 0),
    (1, -1, 0),
    (-1, 1, 0),
    (1, 0, 1),
    (-1, 0, -1),
    (1, 0, -1),
    (-1, 0, 1),
    (0, 1, 1),
    (0, -1, -1),
    (0, 1, -1),
    (0, -1, 1),
]
lattice_weights = [1.0 / 3.0] + [1.0 / 18.0] * 6 + [1.0 / 36.0] * 12
opposite_dir = [0, 2, 1, 4, 3, 6, 5, 8, 7, 10, 9, 12, 11, 14, 13, 16, 15, 18, 17]
omega_rate = 0.9
inlet_speed = 0.05


def with_halo(block, sides, width):
    for axis, dim in sides:
        count = lax.axis_size(axis)
        forward = [(i, i + 1) for i in range(count - 1)]
        backward = [(target, source) for source, target in forward]
        low = lax.ppermute(
            lax.slice_in_dim(block, block.shape[dim] - width, None, axis=dim), axis, forward
        )
        high = lax.ppermute(lax.slice_in_dim(block, 0, width, axis=dim), axis, backward)
        block = jnp.concatenate([low, block, high], axis=dim)
    return block


def equilibrium(density, speeds):
    first, second, third = speeds
    square = first * first + second * second + third * third
    terms = []
    for direction in range(19):
        east, north, upward = lattice_dirs[direction]
        along = east * first + north * second + upward * third
        terms.append(
            lattice_weights[direction]
            * density
            * (1.0 + 3.0 * along + 4.5 * along * along - 1.5 * square)
        )
    return jnp.stack(terms)


def moments(field):
    density = jnp.sum(field, axis=0)
    speeds = []
    for axis_pos in range(3):
        total = jnp.zeros_like(density)
        for direction in range(19):
            factor = lattice_dirs[direction][axis_pos]
            if factor != 0:
                total = total + factor * field[direction]
        speeds.append(total / density)
    return (density, speeds)


def collide(field, kind):
    density, speeds = moments(field)
    relaxed = field - omega_rate * (field - equilibrium(density, speeds))
    unity = jnp.ones_like(density)
    inflow = equilibrium(unity, (inlet_speed * unity, 0.0 * unity, 0.0 * unity))
    return jnp.where(kind == 0, relaxed, jnp.where(kind == 2, inflow, field))


def stream(padded, post, kind_pad, kind):
    width = post.shape[1]
    result = []
    for direction in range(19):
        east, north, upward = lattice_dirs[direction]
        source = jnp.roll(padded[direction, 1 - east : 1 - east + width], (north, upward), (1, 2))
        source_kind = jnp.roll(kind_pad[1 - east : 1 - east + width], (north, upward), (1, 2))
        bounced = jnp.where(source_kind == 1, post[opposite_dir[direction]], source)
        result.append(jnp.where(kind == 1, post[direction], bounced))
    return jnp.stack(result)


def sample(field, kind, phase):
    density, speeds = moments(field)
    speed = jnp.where(kind == 1, 0.0, jnp.stack(speeds))
    shape = speed.shape
    grid = speed.reshape(3, shape[1] // SUB, SUB, shape[2] // SUB, SUB, shape[3] // SUB, SUB)
    grid = lax.dynamic_index_in_dim(grid, phase[2], 6, keepdims=False)
    grid = lax.dynamic_index_in_dim(grid, phase[1], 4, keepdims=False)
    grid = lax.dynamic_index_in_dim(grid, phase[0], 2, keepdims=False)
    return grid


def gram_of(left, right):
    return lax.dot_general(
        left,
        right,
        (((0,), (0,)), ((), ())),
        precision=lax.Precision.HIGHEST,
        preferred_element_type=jnp.float32,
    )


def local(populations, cell_kind, snapshot_order, sample_phase, slab_map, weighted_modes):
    slab_count = lax.axis_size("slab")
    position = lax.axis_index(("group", "slab"))
    group_pos = lax.axis_index("group")
    slab_pos = lax.axis_index("slab")
    width = populations.shape[1]
    channel = 3 * slab_count * width
    kind_pad = with_halo(cell_kind, ((("group", "slab"), 0),), 1)
    planes = position * width - 1 + jnp.arange(width + 2, dtype=jnp.int32)
    outside = (planes < 0) | (planes >= channel)
    kind_pad = jnp.where(outside[:, None, None], 1, kind_pad)
    kind = kind_pad[1:-1]
    field = populations
    samples = []
    for step in range(STEPS):
        post = collide(field, kind)
        padded = with_halo(post, ((("group", "slab"), 1),), 1)
        field = stream(padded, post, kind_pad, kind)
        samples.append(sample(field, kind, sample_phase).reshape(-1))
    chosen = jnp.take(jnp.stack(samples), snapshot_order, axis=0)
    table = jnp.arange(3 * slab_count, dtype=jnp.int32)
    inverse = jnp.sum(jnp.where(slab_map[None, :] == table[:, None], table[None, :], 0), axis=1)
    sources = lax.dynamic_slice_in_dim(inverse, 3 * slab_pos, 3)
    across = lax.all_gather(chosen[None], "group", axis=0, tiled=True)
    everything = lax.all_gather(across[None, :3], "slab", axis=0, tiled=True)
    row_blocks = everything[sources % slab_count, sources // slab_count]
    snaps = jnp.transpose(row_blocks, (0, 2, 1)).reshape(-1, row_blocks.shape[1])
    stacked = jnp.concatenate([weighted_modes, snaps], axis=1)
    gram = lax.psum(gram_of(stacked, stacked), "slab")
    lower = jnp.linalg.cholesky(gram)
    solved = lax.linalg.triangular_solve(
        lower, stacked, left_side=False, lower=True, transpose_a=True
    )
    basis = jnp.where(group_pos == 3, solved * math.sqrt(slab_count * stacked.shape[0]), 0.0)
    lattice = jnp.where(group_pos < 3, field, 0.0)
    return (lattice, basis)


def solution(mesh):
    return jax.shard_map(
        local,
        mesh=mesh,
        in_specs=(
            P(None, ("group", "slab"), None, None),
            P(("group", "slab"), None, None),
            P(),
            P(),
            P(),
            P(("group", "slab"), None),
        ),
        out_specs=(P(None, ("group", "slab"), None, None), P(("group", "slab"), None)),
        check_vma=False,
    )
```

profile of v0, /device:TPU:4, one launch (start us, length us, event | category | flops | bytes accessed | tf_op | source)
XLA Modules:
  0.0 1869.9 jit_solution(17178102112564373106)
XLA Ops:
  8.0 13.3 collective-permute-start.1
  21.3 1.9 collective-permute-start
  25.1 5.3 collective-permute-done
  31.0 1.9 collective-permute-start.2
  32.9 7.9 collective-permute-start.3
  41.0 1.9 collective-permute-done.2
  42.9 1.5 collective-permute-done.3
  46.8 1.9 collective-permute-start.4
  48.8 8.8 collective-permute-start.5
  57.5 2.8 collective-permute-done.4
  64.0 1.9 collective-permute-start.6
  67.1 8.0 collective-permute-start.7
  75.1 2.1 collective-permute-done.6
  77.3 2.0 collective-permute-done.7
  82.4 2.1 collective-permute-start.8
  94.0 2.1 stack.629
  102.7 2.1 stack.633
  110.3 2.1 stack.637
  112.4 8.0 collective-permute-start.9
  133.2 6.7 all_gather.6
  148.8 577.3 %all-gather.3.cloned.1.call-done = f32[384,4,384]{2,1,0:T(4,128)} async-done(((f32[3,4,384]{2,1,0:T(4,128)}), f32[384,4,384]{2,1,0:T(4,128)}) %all-gather.3.cloned.1.call-update) | async-done | bytes 2359312 | tf_op jit(solution)/shard_map/all_gather | solution.py:145
  726.1 2.3 gather_fusion.1
  728.6 3.1 fusion
  732.6 1063.3 %all-reduce.3.cloned.1.call-done = f32[256,256]{0,1:T(8,128)} async-done(((f32[256,256]{0,1:T(8,128)}), f32[256,256]{0,1:T(8,128)}) %all-reduce.3.cloned.1.call-update) | async-done | bytes 262160 | tf_op jit(solution)/shard_map/psum | solution.py:149
  1798.0 11.7 cholesky.50
  1809.8 9.8 custom-call.14
  1820.1 11.9 cholesky.105
  1834.8 4.0 while.1
  1835.4 1.4 bitcast_dynamic-update-slice_fusion.2
  1837.4 1.4 bitcast_dynamic-update-slice_fusion.2
  1838.8 19.7 %custom-call.15 = f32[2,128,128]{1,2,0:T(8,128)S(1)} custom-call(f32[2,128,128]{2,1,0:T(8,128)S(1)} %get-tuple-element.9), custom_call_target="InvertDiagBlocksLowerTriangular" | custom-call | tf_op jit(solution)/shard_map/triangular_solve | solution.py:151
  1861.2 1.4 copy.69
  (491 shorter events, 58.2 us)
Async XLA Ops:
  7.2 17.3 copy-start.1
  7.2 718.9 %all-gather.3.cloned.1.call-start = ((), (), s32[]{:S(2)}) async-start(), calls=%async_computation.1 | async-start | bytes 2377728 | tf_op jit(solution)/shard_map/all_gather | solution.py:145
  8.0 17.1 collective-permute-start.1
  21.3 9.2 collective-permute-start
  31.0 11.9 collective-permute-start.2
  32.9 11.5 collective-permute-start.3
  45.7 34.5 %copy-start.27 = (pred[4,16,128]{2,1,0:T(8,128)(4,1)}, pred[4,16,128]{2,1,0:T(8,128)(4,1)S(1)}, u32[]{:S(2)}) copy-start(pred[4,16,128]{2,1,0:T(8,128)(4,1)S(1)} %get-tuple-element.113) | copy-start | bytes 24580
  45.7 34.5 %copy-start.29 = (pred[4,16,128]{2,1,0:T(8,128)(4,1)}, pred[4,16,128]{2,1,0:T(8,128)(4,1)S(1)}, u32[]{:S(2)}) copy-start(pred[4,16,128]{2,1,0:T(8,128)(4,1)S(1)} %get-tuple-element.115) | copy-start | bytes 24580
  45.7 34.5 %copy-start.31 = (pred[4,16,128]{2,1,0:T(8,128)(4,1)}, pred[4,16,128]{2,1,0:T(8,128)(4,1)S(1)}, u32[]{:S(2)}) copy-start(pred[4,16,128]{2,1,0:T(8,128)(4,1)S(1)} %get-tuple-element.117) | copy-start | bytes 24580
  45.7 34.5 %copy-start.33 = (pred[4,16,128]{2,1,0:T(8,128)(4,1)}, pred[4,16,128]{2,1,0:T(8,128)(4,1)S(1)}, u32[]{:S(2)}) copy-start(pred[4,16,128]{2,1,0:T(8,128)(4,1)S(1)} %get-tuple-element.119) | copy-start | bytes 24580
  45.7 34.5 %copy-start.35 = (pred[4,16,128]{2,1,0:T(8,128)(4,1)}, pred[4,16,128]{2,1,0:T(8,128)(4,1)S(1)}, u32[]{:S(2)}) copy-start(pred[4,16,128]{2,1,0:T(8,128)(4,1)S(1)} %get-tuple-element.121) | copy-start | bytes 24580
  45.7 34.5 %copy-start.37 = (pred[4,16,128]{2,1,0:T(8,128)(4,1)}, pred[4,16,128]{2,1,0:T(8,128)(4,1)S(1)}, u32[]{:S(2)}) copy-start(pred[4,16,128]{2,1,0:T(8,128)(4,1)S(1)} %get-tuple-element.123) | copy-start | bytes 24580
  45.8 34.5 %copy-start.39 = (pred[4,16,128]{2,1,0:T(8,128)(4,1)}, pred[4,16,128]{2,1,0:T(8,128)(4,1)S(1)}, u32[]{:S(2)}) copy-start(pred[4,16,128]{2,1,0:T(8,128)(4,1)S(1)} %get-tuple-element.125) | copy-start | bytes 24580
  45.8 34.5 %copy-start.41 = (pred[4,16,128]{2,1,0:T(8,128)(4,1)}, pred[4,16,128]{2,1,0:T(8,128)(4,1)S(1)}, u32[]{:S(2)}) copy-start(pred[4,16,128]{2,1,0:T(8,128)(4,1)S(1)} %get-tuple-element.127) | copy-start | bytes 24580
  45.8 34.5 %copy-start.43 = (pred[4,16,128]{2,1,0:T(8,128)(4,1)}, pred[4,16,128]{2,1,0:T(8,128)(4,1)S(1)}, u32[]{:S(2)}) copy-start(pred[4,16,128]{2,1,0:T(8,128)(4,1)S(1)} %get-tuple-element.129) | copy-start | bytes 24580
  45.8 34.5 %copy-start.45 = (pred[4,16,128]{2,1,0:T(8,128)(4,1)}, pred[4,16,128]{2,1,0:T(8,128)(4,1)S(1)}, u32[]{:S(2)}) copy-start(pred[4,16,128]{2,1,0:T(8,128)(4,1)S(1)} %get-tuple-element.131) | copy-start | bytes 24580
  45.8 34.5 %copy-start.47 = (pred[4,16,128]{2,1,0:T(8,128)(4,1)}, pred[4,16,128]{2,1,0:T(8,128)(4,1)S(1)}, u32[]{:S(2)}) copy-start(pred[4,16,128]{2,1,0:T(8,128)(4,1)S(1)} %get-tuple-element.133) | copy-start | bytes 24580
  45.8 34.5 %copy-start.49 = (pred[4,16,128]{2,1,0:T(8,128)(4,1)}, pred[4,16,128]{2,1,0:T(8,128)(4,1)S(1)}, u32[]{:S(2)}) copy-start(pred[4,16,128]{2,1,0:T(8,128)(4,1)S(1)} %get-tuple-element.135) | copy-start | bytes 24580
  45.8 34.5 %copy-start.51 = (pred[4,16,128]{2,1,0:T(8,128)(4,1)}, pred[4,16,128]{2,1,0:T(8,128)(4,1)S(1)}, u32[]{:S(2)}) copy-start(pred[4,16,128]{2,1,0:T(8,128)(4,1)S(1)} %get-tuple-element.137) | copy-start | bytes 24580
  45.8 34.5 %copy-start.53 = (pred[4,16,128]{2,1,0:T(8,128)(4,1)}, pred[4,16,128]{2,1,0:T(8,128)(4,1)S(1)}, u32[]{:S(2)}) copy-start(pred[4,16,128]{2,1,0:T(8,128)(4,1)S(1)} %get-tuple-element.139) | copy-start | bytes 24580
  45.8 34.5 %copy-start.55 = (pred[4,16,128]{2,1,0:T(8,128)(4,1)}, pred[4,16,128]{2,1,0:T(8,128)(4,1)S(1)}, u32[]{:S(2)}) copy-start(pred[4,16,128]{2,1,0:T(8,128)(4,1)S(1)} %get-tuple-element.141) | copy-start | bytes 24580
  45.8 34.5 %copy-start.57 = (pred[4,16,128]{2,1,0:T(8,128)(4,1)}, pred[4,16,128]{2,1,0:T(8,128)(4,1)S(1)}, u32[]{:S(2)}) copy-start(pred[4,16,128]{2,1,0:T(8,128)(4,1)S(1)} %get-tuple-element.143) | copy-start | bytes 24580
  46.8 13.6 collective-permute-start.4
  48.8 13.0 collective-permute-start.5
  64.0 13.2 collective-permute-start.6
  67.1 12.2 collective-permute-start.7
  82.4 40.8 %collective-permute-start.8 = (f32[19,1,16,128]{3,2,1,0:T(8,128)}, f32[19,1,16,128]{3,2,1,0:T(8,128)S(1)}, u32[]{:S(2)}, u32[]{:S(2)}) collective-permute-start(f32[19,1,16,128]{3,2,1,0:T(8,128)} %get-tuple-element.197), channel_id=1, source_target_pairs={{0,1},{1,2},{2,3},{3,4},{4,5},{5,6},{6,7},{7,8},{8,9},{9,10},{10,1... | collective-permute-start | bytes 466952 | tf_op jit(solution)/shard_map/ppermute | solution.py:44
  112.4 12.4 collective-permute-start.9
  131.9 16.8 copy-start.18
  132.0 16.8 copy-start.14
  132.1 596.5 %copy-start = (f32[1152,252]{1,0:T(8,128)S(1)}, f32[1152,252]{1,0:T(8,128)}, u32[]{:S(2)}) copy-start(f32[1152,252]{1,0:T(8,128)} %param.11) | copy-start | bytes 3483652
  140.5 1655.4 %all-reduce.3.cloned.1.call-start = ((), (), s32[]{:S(2)}) async-start(), calls=%async_computation | async-start | bytes 524288 | tf_op jit(solution)/shard_map/psum | solution.py:149
  (46 other events, 119.3 us)
Sparse Core Ops, SparseCore 0:
  140.7 585.3 all-gather.2
  731.8 1064.0 all-reduce.2
where the time goes:
time: 1880 us; the launch traced here: 1870 us
  waiting for transfers between devices  1660 us (88%)
  other arithmetic  65.5 us (3%)
  starting transfers between devices  56 us (3%)
  local copies, waits for them, and re-layouts  52.3 us (3%)
  between operations  24.3 us (1%)
    psum x1, waiting for transfers between devices, local(): gram = lax.psum(gram_of(stacked, stacked), 'slab')  1060 us
    all_gather x1, waiting for transfers between devices, local(): everything = lax.all_gather(across[None, :3], 'slab', axis=0, tiled=True)  577 us
    ppermute x5, starting transfers between devices, with_halo(): lax.ppermute(lax.slice_in_dim(block, 0, width, axis=dim), axis, backward)  45.9 us
  transfers between devices with their start and end apart: 12, of which 10 were waited for; matrix products, arithmetic and copies ran while one was open for 2% of the time, Pallas kernels for 0%

commit v1 on v0

v1 whole, which is shorter than its diff:
```python
import functools
import math

import jax
import jax.numpy as jnp
from jax import lax
from jax.experimental import pallas as pl
from jax.experimental.pallas import tpu as pltpu
from jax.sharding import PartitionSpec as P

MESH = pl.DeviceIdType.MESH
STEPS = 4
SUB = 4
OMEGA = 0.9
INLET = 0.05
BIG = 1e30

DIRS = [
    (0, 0, 0),
    (1, 0, 0),
    (-1, 0, 0),
    (0, 1, 0),
    (0, -1, 0),
    (0, 0, 1),
    (0, 0, -1),
    (1, 1, 0),
    (-1, -1, 0),
    (1, -1, 0),
    (-1, 1, 0),
    (1, 0, 1),
    (-1, 0, -1),
    (1, 0, -1),
    (-1, 0, 1),
    (0, 1, 1),
    (0, -1, -1),
    (0, 1, -1),
    (0, -1, 1),
]
WEIGHTS = [1.0 / 3.0] + [1.0 / 18.0] * 6 + [1.0 / 36.0] * 12
OPP = [0, 2, 1, 4, 3, 6, 5, 8, 7, 10, 9, 12, 11, 14, 13, 16, 15, 18, 17]
EAST = [i for i in range(19) if DIRS[i][0] == 1]
WEST = [i for i in range(19) if DIRS[i][0] == -1]
REST = [i for i in range(19) if DIRS[i][0] == 0]

CX, NY, NZ = 4, 16, 128
NLINE = 16
NPLANE = 8
RANK = 256
MODES = 252
ROWS_DEV = 1152


def mm(a, b, dims):
    return lax.dot_general(
        a,
        b,
        (dims, ((), ())),
        precision=lax.Precision.HIGHEST,
        preferred_element_type=jnp.float32,
    )


def inflow_value(i):
    along = DIRS[i][0] * INLET
    return WEIGHTS[i] * (1.0 + 3.0 * along + 4.5 * along * along - 1.5 * INLET * INLET)


def moments(f):
    density = f[0]
    for i in range(1, 19):
        density = density + f[i]
    inverse = 1.0 / density
    speeds = []
    for axis in range(3):
        plus = [f[i] for i in range(19) if DIRS[i][axis] == 1]
        minus = [f[i] for i in range(19) if DIRS[i][axis] == -1]
        total = functools.reduce(lambda a, b: a + b, [a - b for a, b in zip(plus, minus)])
        speeds.append(total * inverse)
    return density, speeds


def collide(f, kind):
    density, u = moments(f)
    square = 1.0 - 1.5 * (u[0] * u[0] + u[1] * u[1] + u[2] * u[2])
    fluid = kind == 0
    inlet = kind == 2
    scaled = {w: (OMEGA * w) * density for w in (1.0 / 3.0, 1.0 / 18.0, 1.0 / 36.0)}
    fallback = {}
    post = [None] * 19
    for i in range(19):
        value = inflow_value(i)
        if value not in fallback:
            fallback[value] = jnp.where(inlet, value, BIG)
    for i in range(19):
        if post[i] is not None:
            continue
        w = scaled[WEIGHTS[i]]
        if i == 0:
            post[0] = jnp.where(fluid, (1.0 - OMEGA) * f[0] + w * square, fallback[inflow_value(0)])
            continue
        along = None
        for axis in range(3):
            if DIRS[i][axis] != 0:
                term = u[axis] if DIRS[i][axis] == 1 else -u[axis]
                along = term if along is None else along + term
        even = w * (square + 4.5 * along * along)
        odd = w * (3.0 * along)
        j = OPP[i]
        post[i] = jnp.where(fluid, (1.0 - OMEGA) * f[i] + (even + odd), fallback[inflow_value(i)])
        post[j] = jnp.where(fluid, (1.0 - OMEGA) * f[j] + (even - odd), fallback[inflow_value(j)])
    return post, u


def shifted(plane, i):
    _, north, upward = DIRS[i]
    if north:
        plane = pltpu.roll(plane, north % NY, 0)
    if upward:
        plane = pltpu.roll(plane, upward % NZ, 1)
    return plane


def first_kernel(
    pop,
    kind_ref,
    phase,
    order,
    table,
    modes,
    field,
    gram_out,
    cross_out,
    self_out,
    snaps_out,
    east,
    west,
    rest,
    speeds,
    samples,
    message,
    line,
    staging,
    picks,
    landed,
    gpart,
    slot_a,
    slot_b,
    rows_a,
    rows_b,
    cross_own,
    cross_a,
    cross_mid,
    cross_b,
    halo_send,
    halo_recv,
    line_send,
    line_recv,
    route_send,
    route_recv,
    ga_send,
    ga_recv,
    gb_send,
    gb_recv,
    gd_send,
    gd_recv,
    ca_send,
    ca_recv,
    cb_send,
    cb_recv,
):
    group = lax.axis_index("group")
    slab = lax.axis_index("slab")
    zpos = slab // NPLANE
    ppos = slab % NPLANE
    position = group * 128 + slab
    channel = group < 3
    has_west = jnp.logical_and(channel, position > 0)
    has_east = jnp.logical_and(channel, position < 383)
    west_id = ((position - 1) // 128, (position + 127) % 128)
    east_id = ((position + 1) // 128, (position + 1) % 128)

    barrier = pltpu.get_barrier_semaphore()

    def hello(target):
        pl.semaphore_signal(barrier, inc=1, device_id=target, device_id_type=MESH)

    def line_peer(d):
        return (group, ((zpos + d) % NLINE) * NPLANE + ppos)

    def greet_line(d, c):
        hello(line_peer(d))
        return c

    lax.fori_loop(1, NLINE, greet_line, 0)

    def gather_plane(post, x, store_slot):
        for n, i in enumerate(EAST):
            east[store_slot, x + 1, n] = post[i]
        for n, i in enumerate(WEST):
            west[store_slot, x + 1, n] = post[i]
        for n, i in enumerate(REST):
            rest[store_slot, x, n] = post[i]

    def streamed(slot, x):
        f = [None] * 19
        for n, i in enumerate(REST):
            if i == 0:
                f[0] = rest[slot, x, 0]
                continue
            source = shifted(rest[slot, x, n], i)
            f[i] = jnp.where(source >= 0.5 * BIG, rest[slot, x, REST.index(OPP[i])], source)
        for n, i in enumerate(EAST):
            source = shifted(east[slot, x, n], i)
            f[i] = jnp.where(source >= 0.5 * BIG, west[slot, x + 1, WEST.index(OPP[i])], source)
        for n, i in enumerate(WEST):
            source = shifted(west[slot, x + 2, n], i)
            f[i] = jnp.where(source >= 0.5 * BIG, east[slot, x + 1, EAST.index(OPP[i])], source)
        return f

    def keep_speeds(u, kind, x):
        for c in range(3):
            speeds[x, c] = jnp.where(kind == 1, 0.0, u[c])

    def halo(slot):
        go_east = pltpu.make_async_remote_copy(
            src_ref=east.at[slot, CX],
            dst_ref=east.at[slot, 0],
            send_sem=halo_send.at[slot, 0],
            recv_sem=halo_recv.at[slot, 0],
            device_id=east_id,
            device_id_type=MESH,
        )
        go_west = pltpu.make_async_remote_copy(
            src_ref=west.at[slot, 1],
            dst_ref=west.at[slot, CX + 1],
            send_sem=halo_send.at[slot, 1],
            recv_sem=halo_recv.at[slot, 1],
            device_id=west_id,
            device_id_type=MESH,
        )
        return go_east, go_west

    def send_halo(slot):
        go_east, go_west = halo(slot)

        @pl.when(has_east)
        def _():
            go_east.start()

        @pl.when(has_west)
        def _():
            go_west.start()

    def take_halo(slot):
        go_east, go_west = halo(slot)

        @pl.when(has_west)
        def _():
            go_east.wait_recv()

        @pl.when(has_east)
        def _():
            go_west.wait_recv()

    def first_plane(x):
        kind = kind_ref[x]
        post, _ = collide([pop[i, x] for i in range(19)], kind)
        gather_plane(post, x, 0)

    def middle_plane(slot, x):
        kind = kind_ref[x]
        f = streamed(slot, x)
        post, u = collide(f, kind)
        keep_speeds(u, kind, x)
        gather_plane(post, x, slot + 1)

    def last_plane(slot, x):
        kind = kind_ref[x]
        f = streamed(slot, x)
        _, u = moments(f)
        keep_speeds(u, kind, x)
        for i in range(19):
            field[i, x] = jnp.where(kind == 1, pop[i, x], f[i])

    @pl.when(channel)
    def _():
        @pl.when(has_east)
        def _():
            hello(east_id)

        @pl.when(has_west)
        def _():
            hello(west_id)

        def greet_analysis(p, c):
            hello((3, zpos * NPLANE + p))
            return c

        lax.fori_loop(0, NPLANE, greet_analysis, 0)

        samples[...] = jnp.zeros((STEPS, 8, NZ), jnp.float32)

        @pl.when(position == 0)
        def _():
            east[:, 0] = jnp.full((STEPS, 5, NY, NZ), BIG, jnp.float32)

        @pl.when(position == 383)
        def _():
            west[:, CX + 1] = jnp.full((STEPS, 5, NY, NZ), BIG, jnp.float32)

        def edges_first(n, c):
            first_plane(3 * n)
            return c

        lax.fori_loop(0, 2, edges_first, 0)
        edge = jnp.logical_or(position == 0, position == 383)

        @pl.when(edge)
        def _():
            pl.semaphore_wait(barrier, 15 + 8 + 1)

        @pl.when(jnp.logical_not(edge))
        def _():
            pl.semaphore_wait(barrier, 15 + 8 + 2)

        send_halo(0)

        def inner_first(n, c):
            first_plane(1 + n)
            return c

        lax.fori_loop(0, 2, inner_first, 0)

        def pick(q, c):
            found = jnp.int32(-1)
            for z in range(NLINE):
                row = table[group * 128 + z * NPLANE + ppos]
                found = jnp.where(row == 24 * zpos + q, z, found)
            picks[q] = found
            return c

        lax.fori_loop(0, 24, pick, 0)

        lanes = lax.broadcasted_iota(jnp.int32, (NZ, NZ), 1)
        depth = lax.broadcasted_iota(jnp.int32, (NZ, NZ), 0)
        pick_z = (depth == phase[2] + SUB * (lanes % 32)).astype(jnp.float32)
        lane3 = lax.broadcasted_iota(jnp.int32, (3, NY, NZ), 2)
        row3 = lax.broadcasted_iota(jnp.int32, (3, NY, NZ), 1)
        pick_y = row3 == phase[1] + SUB * (lane3 // 32)

        def sample(step):
            plane = speeds[phase[0]].reshape(3 * NY, NZ)
            along = mm(plane, pick_z, ((1,), (0,))).reshape(3, NY, NZ)
            samples[step, 0:3] = jnp.sum(jnp.where(pick_y, along, 0.0), axis=1)

        def one_step(slot, c):
            def inner(n, c):
                middle_plane(slot, 1 + n)
                return c

            lax.fori_loop(0, 2, inner, 0)
            take_halo(slot)

            def edges(n, c):
                middle_plane(slot, 3 * n)
                return c

            lax.fori_loop(0, 2, edges, 0)
            send_halo(slot + 1)
            sample(slot)
            return c

        lax.fori_loop(0, STEPS - 1, one_step, 0)

        def inner_last(n, c):
            last_plane(STEPS - 1, 1 + n)
            return c

        lax.fori_loop(0, 2, inner_last, 0)
        take_halo(STEPS - 1)

        def edges_last(n, c):
            last_plane(STEPS - 1, 3 * n)
            return c

        lax.fori_loop(0, 2, edges_last, 0)
        sample(STEPS - 1)

        for k in range(STEPS):
            message[4 * k : 4 * k + 4] = samples[order[k], 0:4]
        line[zpos] = message[...]

        def send_line(d, c):
            pltpu.make_async_remote_copy(
                src_ref=message,
                dst_ref=line.at[zpos],
                send_sem=line_send,
                recv_sem=line_recv,
                device_id=line_peer(d),
                device_id_type=MESH,
            ).start()
            return c

        lax.fori_loop(1, NLINE, send_line, 0)
        pltpu.make_async_copy(line.at[0:15], line.at[0:15], line_recv).wait()

        def place(q, c):
            z = picks[q]
            block = line[jnp.maximum(z, 0)]
            staging[q] = jnp.where(z >= 0, block, 0.0)
            return c

        lax.fori_loop(0, 24, place, 0)

        def send_route(p, c):
            pltpu.make_async_remote_copy(
                src_ref=staging.at[pl.ds(3 * p, 3)],
                dst_ref=landed.at[group * NPLANE + ppos],
                send_sem=route_send,
                recv_sem=route_recv,
                device_id=(3, zpos * NPLANE + p),
                device_id_type=MESH,
            ).start()
            return c

        lax.fori_loop(0, NPLANE, send_route, 0)

        def sent(slot, c):
            go_east, go_west = halo(slot)

            @pl.when(has_east)
            def _():
                go_east.wait_send()

            @pl.when(has_west)
            def _():
                go_west.wait_send()

            return c

        lax.fori_loop(0, STEPS, sent, 0)
        pltpu.make_async_copy(line.at[0:15], line.at[0:15], line_send).wait()
        pltpu.make_async_copy(staging, staging, route_send).wait()

    @pl.when(jnp.logical_not(channel))
    def _():
        def greet_channel(n, c):
            hello((n // NPLANE, zpos * NPLANE + n % NPLANE))
            return c

        lax.fori_loop(0, 24, greet_channel, 0)

        def plane_peer(d):
            return (3, zpos * NPLANE + (ppos + d) % NPLANE)

        def greet_plane(d, c):
            hello(plane_peer(d))
            return c

        lax.fori_loop(1, NPLANE, greet_plane, 0)

        part = mm(modes[...], modes[...], ((0,), (0,)))
        gpart[...] = jnp.zeros((NLINE, 16, RANK), jnp.float32)
        for n in range(NLINE):
            count = min(16, MODES - 16 * n)
            gpart[n, 0:count, 0:MODES] = part[16 * n : 16 * n + count]
        pl.semaphore_wait(barrier, 15 + 24 + 7)

        slot_a[zpos] = gpart[zpos]

        def send_a(d, c):
            pltpu.make_async_remote_copy(
                src_ref=gpart.at[(zpos + d) % NLINE],
                dst_ref=slot_a.at[zpos],
                send_sem=ga_send,
                recv_sem=ga_recv,
                device_id=line_peer(d),
                device_id_type=MESH,
            ).start()
            return c

        lax.fori_loop(1, NLINE, send_a, 0)
        pltpu.make_async_copy(slot_a.at[0:15], slot_a.at[0:15], ga_recv).wait()
        rows_a[...] = jnp.sum(slot_a[...], axis=0)
        slot_b[ppos] = rows_a[...]

        def send_b(d, c):
            pltpu.make_async_remote_copy(
                src_ref=rows_a,
                dst_ref=slot_b.at[ppos],
                send_sem=gb_send,
                recv_sem=gb_recv,
                device_id=plane_peer(d),
                device_id_type=MESH,
            ).start()
            return c

        lax.fori_loop(1, NPLANE, send_b, 0)
        pltpu.make_async_copy(slot_b.at[0:7], slot_b.at[0:7], gb_recv).wait()
        rows_b[...] = jnp.sum(slot_b[...], axis=0)
        gram_out[zpos] = rows_b[...]

        def send_d(d, c):
            pltpu.make_async_remote_copy(
                src_ref=rows_b,
                dst_ref=gram_out.at[zpos],
                send_sem=gd_send,
                recv_sem=gd_recv,
                device_id=line_peer(d),
                device_id_type=MESH,
            ).start()
            return c

        lax.fori_loop(1, NLINE, send_d, 0)
        pltpu.make_async_copy(gram_out.at[0:15], gram_out.at[0:15], gd_recv).wait()

        pltpu.make_async_copy(landed, landed, route_recv).wait()
        total = landed[0]
        for n in range(1, 24):
            total = total + landed[n]
        snaps = jnp.concatenate(
            [
                jnp.concatenate([total[t, 4 * k + c : 4 * k + c + 1] for k in range(4)], axis=0)
                for t in range(3)
                for c in range(3)
            ],
            axis=1,
        )
        snaps_out[0:4] = snaps
        snaps_out[4:8] = jnp.zeros((4, ROWS_DEV), jnp.float32)
        whole = snaps_out[...]
        cross_own[0, :, 0:MODES] = mm(whole, modes[...], ((1,), (0,)))
        cross_own[0, :, MODES:RANK] = jnp.zeros((8, RANK - MODES), jnp.float32)
        cross_own[1] = jnp.zeros((8, RANK), jnp.float32)
        cross_own[1, :, 0:8] = mm(whole, whole, ((1,), (1,)))
        cross_a[zpos] = cross_own[...]

        def send_ca(d, c):
            pltpu.make_async_remote_copy(
                src_ref=cross_own,
                dst_ref=cross_a.at[zpos],
                send_sem=ca_send,
                recv_sem=ca_recv,
                device_id=line_peer(d),
                device_id_type=MESH,
            ).start()
            return c

        lax.fori_loop(1, NLINE, send_ca, 0)
        pltpu.make_async_copy(cross_a.at[0:15], cross_a.at[0:15], ca_recv).wait()
        cross_mid[...] = jnp.sum(cross_a[...], axis=0)
        cross_b[ppos] = cross_mid[...]

        def send_cb(d, c):
            pltpu.make_async_remote_copy(
                src_ref=cross_mid,
                dst_ref=cross_b.at[ppos],
                send_sem=cb_send,
                recv_sem=cb_recv,
                device_id=plane_peer(d),
                device_id_type=MESH,
            ).start()
            return c

        lax.fori_loop(1, NPLANE, send_cb, 0)
        pltpu.make_async_copy(cross_b.at[0:7], cross_b.at[0:7], cb_recv).wait()
        both = jnp.sum(cross_b[...], axis=0)
        cross_out[...] = both[0]
        self_out[...] = both[1]

        pltpu.make_async_copy(slot_a.at[0:15], slot_a.at[0:15], ga_send).wait()
        pltpu.make_async_copy(slot_b.at[0:7], slot_b.at[0:7], gb_send).wait()
        pltpu.make_async_copy(gram_out.at[0:15], gram_out.at[0:15], gd_send).wait()
        pltpu.make_async_copy(cross_a.at[0:15], cross_a.at[0:15], ca_send).wait()
        pltpu.make_async_copy(cross_b.at[0:7], cross_b.at[0:7], cb_send).wait()


def lower_half(error, row, col):
    return jnp.where(row > col, error, jnp.where(row == col, 0.5 * error, 0.0))


def second_kernel(field, modes, gram, cross, self_ref, snaps, lattice, basis, scaled, inverse, left, pivots):
    group = lax.axis_index("group")

    @pl.when(group < 3)
    def _():
        lattice[...] = field[...]
        basis[...] = jnp.zeros((ROWS_DEV, RANK), jnp.float32)

    @pl.when(group == 3)
    def _():
        lattice[...] = jnp.zeros((19, CX, NY, NZ), jnp.float32)
        row = lax.broadcasted_iota(jnp.int32, (RANK, RANK), 0)
        col = lax.broadcasted_iota(jnp.int32, (RANK, RANK), 1)
        eye = (row == col).astype(jnp.float32)
        pad = jnp.logical_and(row == col, row >= MODES)
        whole = jnp.where(pad, 1.0, gram[...].reshape(RANK, RANK))
        diagonal = jnp.where(row == col, whole, 0.0)
        rs_row = 1.0 / jnp.sqrt(jnp.sum(diagonal, axis=0, keepdims=True))
        rs_col = 1.0 / jnp.sqrt(jnp.sum(diagonal, axis=1, keepdims=True))
        scaled[...] = whole * rs_row * rs_col
        inverse[...] = eye - lower_half(scaled[...] - eye, row, col)

        def go_on(state):
            count, size = state
            return jnp.logical_and(count < 6, jnp.logical_not(size < 1e-6))

        def newton(state):
            count, _ = state
            here = inverse[...]
            error = mm(mm(here, scaled[...], ((1,), (0,))), here, ((1,), (1,))) - eye
            inverse[...] = here - mm(lower_half(error, row, col), here, ((1,), (0,)))
            return count + 1, jnp.sum(error * error)

        _, size = lax.while_loop(go_on, newton, (jnp.int32(0), jnp.float32(1.0)))

        @pl.when(jnp.logical_not(size < 1e-6))
        def _():
            left[...] = scaled[...]
            inverse[...] = eye
            pivots[...] = jnp.ones((RANK, 128), jnp.float32)

            def eliminate(j, c):
                line = left[pl.ds(j, 1), :]
                mine = inverse[pl.ds(j, 1), :]
                lane = lax.broadcasted_iota(jnp.int32, (1, RANK), 1)
                pivot = jnp.sum(jnp.where(lane == j, line, 0.0), axis=1, keepdims=True)
                column = jnp.sum(jnp.where(col == j, left[...], 0.0), axis=1, keepdims=True)
                below = lax.broadcasted_iota(jnp.int32, (RANK, 1), 0) > j
                factor = jnp.where(below, column / pivot, 0.0)
                left[...] = left[...] - factor * line
                inverse[...] = inverse[...] - factor * mine
                pivots[pl.ds(j, 1), :] = jnp.broadcast_to(pivot, (1, 128))
                return c

            lax.fori_loop(0, RANK, eliminate, 0)
            inverse[...] = inverse[...] / jnp.sqrt(pivots[:, 0:1])

        factor = inverse[...] * rs_row
        tail = mm(cross[...], factor, ((1,), (1,)))
        rest = self_ref[:, 0:8] - mm(tail, tail, ((1,), (1,)))
        lane = lax.broadcasted_iota(jnp.int32, (8, RANK), 1)
        sub = lax.broadcasted_iota(jnp.int32, (8, RANK), 0)
        unit = (lane == MODES + sub).astype(jnp.float32)
        right = unit - mm(tail, factor, ((1,), (0,)))
        entry = [[rest[i : i + 1, j : j + 1] for j in range(4)] for i in range(4)]
        low = [[None] * 4 for _ in range(4)]
        lines = []
        for i in range(4):
            for j in range(i + 1):
                value = entry[i][j]
                for k in range(j):
                    value = value - low[i][k] * low[j][k]
                low[i][j] = jnp.sqrt(value) if i == j else value / low[j][j]
            line = right[i : i + 1]
            for k in range(i):
                line = line - low[i][k] * lines[k]
            lines.append(line / low[i][i])
        inverse[...] = factor
        inverse[MODES:RANK] = jnp.concatenate(lines, axis=0)
        scale = math.sqrt(128 * ROWS_DEV)
        final = inverse[...] * scale
        first = final[:, 0:MODES]
        second = jnp.concatenate([final[MODES:RANK, MODES:RANK], jnp.zeros((4, 4), jnp.float32)], axis=0)
        second = jnp.concatenate([second, jnp.zeros((8, 4), jnp.float32)], axis=1)
        placed = mm(second, unit[:, 128:RANK], ((0,), (0,)))

        for n in range(9):
            block = pl.ds(128 * n, 128)
            out = mm(modes[block, :], first, ((1,), (1,)))
            mine = snaps[:, 128 * n : 128 * (n + 1)]
            basis[block, 0:128] = out[:, 0:128]
            basis[block, 128:RANK] = out[:, 128:RANK] + mm(mine, placed, ((0,), (0,)))


def local(populations, cell_kind, snapshot_order, sample_phase, slab_map, weighted_modes):
    f32 = jnp.float32
    vmem = pl.BlockSpec(memory_space=pltpu.VMEM)
    smem = pl.BlockSpec(memory_space=pltpu.SMEM)
    dma = pltpu.SemaphoreType.DMA
    field, gram, cross, own, snaps = pl.pallas_call(
        first_kernel,
        out_shape=(
            jax.ShapeDtypeStruct((19, CX, NY, NZ), f32),
            jax.ShapeDtypeStruct((NLINE, 16, RANK), f32),
            jax.ShapeDtypeStruct((8, RANK), f32),
            jax.ShapeDtypeStruct((8, RANK), f32),
            jax.ShapeDtypeStruct((8, ROWS_DEV), f32),
        ),
        in_specs=[vmem, vmem, smem, smem, smem, vmem],
        out_specs=(vmem,) * 5,
        scratch_shapes=[
            pltpu.VMEM((STEPS, CX + 2, 5, NY, NZ), f32),
            pltpu.VMEM((STEPS, CX + 2, 5, NY, NZ), f32),
            pltpu.VMEM((STEPS, CX, 9, NY, NZ), f32),
            pltpu.VMEM((CX, 3, NY, NZ), f32),
            pltpu.VMEM((STEPS, 8, NZ), f32),
            pltpu.VMEM((16, NZ), f32),
            pltpu.VMEM((NLINE, 16, NZ), f32),
            pltpu.VMEM((24, 16, NZ), f32),
            pltpu.SMEM((24,), jnp.int32),
            pltpu.VMEM((24, 3, 16, NZ), f32),
            pltpu.VMEM((NLINE, 16, RANK), f32),
            pltpu.VMEM((NLINE, 16, RANK), f32),
            pltpu.VMEM((NPLANE, 16, RANK), f32),
            pltpu.VMEM((16, RANK), f32),
            pltpu.VMEM((16, RANK), f32),
            pltpu.VMEM((2, 8, RANK), f32),
            pltpu.VMEM((NLINE, 2, 8, RANK), f32),
            pltpu.VMEM((2, 8, RANK), f32),
            pltpu.VMEM((NPLANE, 2, 8, RANK), f32),
            dma((STEPS, 2)),
            dma((STEPS, 2)),
        ]
        + [dma] * 14,
        compiler_params=pltpu.CompilerParams(
            collective_id=0, has_side_effects=True, vmem_limit_bytes=32 * 1024 * 1024
        ),
    )(populations, cell_kind, sample_phase, snapshot_order, slab_map, weighted_modes)
    return pl.pallas_call(
        second_kernel,
        out_shape=(
            jax.ShapeDtypeStruct((19, CX, NY, NZ), f32),
            jax.ShapeDtypeStruct((ROWS_DEV, RANK), f32),
        ),
        in_specs=[vmem] * 6,
        out_specs=(vmem, vmem),
        scratch_shapes=[
            pltpu.VMEM((RANK, RANK), f32),
            pltpu.VMEM((RANK, RANK), f32),
            pltpu.VMEM((RANK, RANK), f32),
            pltpu.VMEM((RANK, 128), f32),
        ],
        compiler_params=pltpu.CompilerParams(vmem_limit_bytes=32 * 1024 * 1024),
    )(field, weighted_modes, gram, cross, own, snaps)


def solution(mesh):
    return jax.shard_map(
        local,
        mesh=mesh,
        in_specs=(
            P(None, ("group", "slab"), None, None),
            P(("group", "slab"), None, None),
            P(),
            P(),
            P(),
            P(("group", "slab"), None),
        ),
        out_specs=(P(None, ("group", "slab"), None, None), P(("group", "slab"), None)),
        check_vma=False,
    )
```

time: 1880 us -> 127 us (0.07)
  the two profiles are of different devices: /device:TPU:4 before, /device:TPU:7 now
where the time goes in v1:
time: 127 us
  Pallas kernels  121 us (95%)
  local copies, waits for them, and re-layouts  5.09 us (4%)
    pallas_call x1, Pallas kernels, local(): pl.pallas_call(first_kernel, out_shape=(jax.ShapeDtypeStruct((19, CX, NY,...  70.4 us
    pallas_call x1, Pallas kernels, local(): pl.pallas_call(second_kernel, out_shape=(jax.ShapeDtypeStruct((19, CX, NY...  50.5 us
    unnamed x14, local copies, waits for them, and re-layouts  5.09 us

profile of v1, /device:TPU:7, one launch (start us, length us, event | category | flops | bytes accessed | tf_op | source)
XLA Modules:
  0.0 126.6 jit_solution(13906874944191873956)
XLA Ops:
  0.6 0.0 copy-start
  0.6 1.3 copy-done
  1.9 0.0 copy-start.2
  1.9 1.1 copy-done.2
  3.0 0.0 copy-start.3
  3.0 0.8 copy-done.3
  3.7 0.0 copy-start.4
  3.7 0.7 copy-done.4
  4.4 0.0 copy-start.5
  4.4 0.7 copy-done.5
  5.1 0.0 copy-start.6
  5.1 0.7 copy-done.6
  5.7 0.0 copy-start.1
  5.7 70.4 %shard_map.77 = (f32[19,4,16,128]{3,2,1,0:T(8,128)S(1)}, f32[16,16,256]{2,1,0:T(8,128)S(1)}, f32[8,256]{1,0:T(8,128)S(1)}, f32[8,256]{1,0:T(8,128)S(1)}, f32[8,1152]{1,0:T(8,128)S(1)}) custom-call(f32[19,4,16,128]{3,2,1,0:T(8,128)S(1)} %copy-done.2, s32[4,16,128]{2,1,0:T(8,128)S(1)} %copy-done.3, s32[3]{0:T(128)S(1)} %copy-done.5, s32[4]{0:T(128)S(1)} %copy-done.6, ...), custom_call_target="tpu_custom_call" | custom-call | tf_op jit(solution)/shard_map/pallas_call | solution.py:681
  76.1 0.0 copy-done.1
  76.1 50.5 %shard_map.78 = (f32[19,4,16,128]{3,2,1,0:T(8,128)}, f32[1152,256]{1,0:T(8,128)}) custom-call(f32[19,4,16,128]{3,2,1,0:T(8,128)S(1)} %get-tuple-element.7.field, f32[1152,252]{1,0:T(8,128)S(1)} %copy-done.1, f32[16,16,256]{2,1,0:T(8,128)S(1)} %get-tuple-element.8.gram, f32[8,256]{1,0:T(8,128)S(1)} %get-tuple-element.9.cross, ...), custom_call_target="tpu_custom_call" | custom-call | tf_op jit(solution)/shard_map/pallas_call | solution.py:720
Async XLA Ops:
  0.6 1.3 %copy-start = (f32[1152,252]{1,0:T(8,128)S(1)}, f32[1152,252]{1,0:T(8,128)}, u32[]{:S(2)}) copy-start(f32[1152,252]{1,0:T(8,128)} %modes.3) | copy-start | bytes 3483652
  1.9 1.1 copy-start.2
  3.0 0.8 copy-start.3
  3.7 0.7 copy-start.4
  4.4 0.7 copy-start.5
  5.1 0.7 copy-start.6
  5.7 70.4 %copy-start.1 = (f32[1152,252]{1,0:T(8,128)S(1)}, f32[1152,252]{1,0:T(8,128)}, u32[]{:S(2)}) copy-start(f32[1152,252]{1,0:T(8,128)} %modes.3) | copy-start | bytes 3483652

commit v2 on v1

v2 whole, which is shorter than its diff:
```python
import functools
import math

import jax
import jax.numpy as jnp
from jax import lax
from jax.experimental import pallas as pl
from jax.experimental.pallas import tpu as pltpu
from jax.sharding import PartitionSpec as P

MESH = pl.DeviceIdType.MESH
STEPS = 4
SUB = 4
OMEGA = 0.9
INLET = 0.05
BIG = 1e30

DIRS = [
    (0, 0, 0),
    (1, 0, 0),
    (-1, 0, 0),
    (0, 1, 0),
    (0, -1, 0),
    (0, 0, 1),
    (0, 0, -1),
    (1, 1, 0),
    (-1, -1, 0),
    (1, -1, 0),
    (-1, 1, 0),
    (1, 0, 1),
    (-1, 0, -1),
    (1, 0, -1),
    (-1, 0, 1),
    (0, 1, 1),
    (0, -1, -1),
    (0, 1, -1),
    (0, -1, 1),
]
WEIGHTS = [1.0 / 3.0] + [1.0 / 18.0] * 6 + [1.0 / 36.0] * 12
OPP = [0, 2, 1, 4, 3, 6, 5, 8, 7, 10, 9, 12, 11, 14, 13, 16, 15, 18, 17]
EAST = [i for i in range(19) if DIRS[i][0] == 1]
WEST = [i for i in range(19) if DIRS[i][0] == -1]
REST = [i for i in range(19) if DIRS[i][0] == 0]

CX, NY, NZ = 4, 16, 128
NLINE = 16
NPLANE = 8
RANK = 256
MODES = 252
ROWS_DEV = 1152
ROWS_ALL = 128 * ROWS_DEV
SCALE = math.sqrt(ROWS_ALL)
NEWTON = 3
ROOM = 60 * 1024 * 1024
LINE_FAR = [8, 7, 9, 6, 10, 5, 11, 4, 12, 3, 13, 2, 14, 1, 15]
PLANE_FAR = [4, 5, 3, 6, 2, 7, 1]


def mm(a, b, dims):
    return lax.dot_general(
        a,
        b,
        (dims, ((), ())),
        precision=lax.Precision.HIGHEST,
        preferred_element_type=jnp.float32,
    )


def inflow_value(i):
    along = DIRS[i][0] * INLET
    return WEIGHTS[i] * (1.0 + 3.0 * along + 4.5 * along * along - 1.5 * INLET * INLET)


def moments(f):
    density = f[0]
    for i in range(1, 19):
        density = density + f[i]
    inverse = 1.0 / density
    speeds = []
    for axis in range(3):
        plus = [f[i] for i in range(19) if DIRS[i][axis] == 1]
        minus = [f[i] for i in range(19) if DIRS[i][axis] == -1]
        total = functools.reduce(lambda a, b: a + b, [a - b for a, b in zip(plus, minus)])
        speeds.append(total * inverse)
    return density, speeds


def collide(f, kind):
    density, u = moments(f)
    square = 1.0 - 1.5 * (u[0] * u[0] + u[1] * u[1] + u[2] * u[2])
    fluid = kind == 0
    inlet = kind == 2
    scaled = {w: (OMEGA * w) * density for w in (1.0 / 3.0, 1.0 / 18.0, 1.0 / 36.0)}
    fallback = {}
    post = [None] * 19
    for i in range(19):
        value = inflow_value(i)
        if value not in fallback:
            fallback[value] = jnp.where(inlet, value, BIG)
    for i in range(19):
        if post[i] is not None:
            continue
        w = scaled[WEIGHTS[i]]
        if i == 0:
            post[0] = jnp.where(fluid, (1.0 - OMEGA) * f[0] + w * square, fallback[inflow_value(0)])
            continue
        along = None
        for axis in range(3):
            if DIRS[i][axis] != 0:
                term = u[axis] if DIRS[i][axis] == 1 else -u[axis]
                along = term if along is None else along + term
        even = w * (square + 4.5 * along * along)
        odd = w * (3.0 * along)
        j = OPP[i]
        post[i] = jnp.where(fluid, (1.0 - OMEGA) * f[i] + (even + odd), fallback[inflow_value(i)])
        post[j] = jnp.where(fluid, (1.0 - OMEGA) * f[j] + (even - odd), fallback[inflow_value(j)])
    return post, u


def shifted(plane, i):
    _, north, upward = DIRS[i]
    if north:
        plane = pltpu.roll(plane, north % NY, 0)
    if upward:
        plane = pltpu.roll(plane, upward % NZ, 1)
    return plane


def lower_half(error, row, col):
    return jnp.where(row > col, error, jnp.where(row == col, 0.5 * error, 0.0))


def square_iota():
    row = lax.broadcasted_iota(jnp.int32, (RANK, RANK), 0)
    col = lax.broadcasted_iota(jnp.int32, (RANK, RANK), 1)
    return row, col, (row == col).astype(jnp.float32)


def unit_diagonal(gram):
    row, col, _ = square_iota()
    whole = jnp.where(jnp.logical_and(row == col, row >= MODES), 1.0, gram)
    diagonal = jnp.where(row == col, whole, 0.0)
    along_row = jnp.sum(diagonal, axis=0, keepdims=True)
    rs_row = 1.0 / jnp.sqrt(along_row)
    rs_col = 1.0 / jnp.sqrt(jnp.sum(diagonal, axis=1, keepdims=True))
    return whole * rs_row * rs_col, rs_row, along_row


def last_columns(lines, is_step):
    lane = lax.broadcasted_iota(jnp.int32, (1, RANK), 1)
    old = [jnp.where(lane < MODES, line, 0.0) for line in lines]
    gram = [[None] * 4 for _ in range(4)]
    for s in range(4):
        for t in range(s + 1):
            own = jnp.where(lane == MODES + t, lines[s], 0.0)
            gram[s][t] = jnp.sum(own - old[s] * old[t] * (1.0 / ROWS_ALL), axis=1, keepdims=True)
            gram[t][s] = gram[s][t]

    def chosen(k, values):
        result = values[3]
        for s in range(3):
            result = jnp.where(is_step(k, s), values[s], result)
        return result

    half = [[chosen(k, [gram[s][t] for s in range(4)]) for t in range(4)] for k in range(4)]
    entry = [[chosen(j, half[k]) for j in range(k + 1)] for k in range(4)]
    start = []
    for s in range(4):
        start.append(SCALE * (lane == MODES + s).astype(jnp.float32) - old[s] * (SCALE / ROWS_ALL))
    low = [[None] * 4 for _ in range(4)]
    result = []
    for k in range(4):
        for j in range(k + 1):
            value = entry[k][j]
            for m in range(j):
                value = value - low[k][m] * low[j][m]
            low[k][j] = jnp.sqrt(value) if k == j else value / low[j][j]
        line = chosen(k, start)
        for m in range(k):
            line = line - low[k][m] * result[m]
        result.append(line / low[k][k])
    return result


def first_kernel(
    pop_hbm,
    kind_hbm,
    phase_hbm,
    order_hbm,
    table_hbm,
    modes_hbm,
    field_hbm,
    gram_hbm,
    q_hbm,
    small_hbm,
    field,
    gram,
    q,
    small,
    pop,
    kind_ref,
    phase,
    order,
    table,
    modes,
    east,
    west,
    rest,
    speeds,
    samples,
    early,
    line_a,
    line_b,
    staging_a,
    staging_b,
    picks,
    landed_a,
    landed_b,
    gpart,
    slot_a,
    slot_b,
    rows_a,
    rows_b,
    scaled,
    inverse,
    snaps,
    cross_own,
    cross_a,
    cross_mid,
    cross_b,
    load_sem,
    store_sem,
    halo_send,
    halo_recv,
    send_sem,
    recv_sem,
):
    group = lax.axis_index("group")
    slab = lax.axis_index("slab")
    zpos = slab // NPLANE
    ppos = slab % NPLANE
    position = group * 128 + slab
    channel = group < 3
    has_west = jnp.logical_and(channel, position > 0)
    has_east = jnp.logical_and(channel, position < 383)
    west_id = ((position - 1) // 128, (position + 127) % 128)
    east_id = ((position + 1) // 128, (position + 1) % 128)
    LINE_A, LINE_B, ROUTE_A, ROUTE_B, GRAM_A, GRAM_B, GRAM_D, CROSS_A, CROSS_B = range(9)

    barrier = pltpu.get_barrier_semaphore()

    def hello(target):
        pl.semaphore_signal(barrier, inc=1, device_id=target, device_id_type=MESH)

    loads = [
        pltpu.make_async_copy(a, b, load_sem.at[n])
        for n, (a, b) in enumerate(
            [
                (pop_hbm, pop),
                (kind_hbm, kind_ref),
                (phase_hbm, phase),
                (table_hbm, table),
                (order_hbm, order),
                (modes_hbm, modes),
            ]
        )
    ]

    stores = [
        pltpu.make_async_copy(a, b, store_sem.at[n])
        for n, (a, b) in enumerate(
            [
                (field, field_hbm),
                (gram, gram_hbm),
                (q.at[:, 0:128], q_hbm.at[:, 0:128]),
                (q.at[:, 128:RANK], q_hbm.at[:, 128:RANK]),
                (small, small_hbm),
            ]
        )
    ]

    @pl.when(channel)
    def _():
        for n in range(4):
            loads[n].start()

    @pl.when(jnp.logical_not(channel))
    def _():
        loads[5].start()
        loads[4].start()

    def line_peer(d):
        return (group, ((zpos + d) % NLINE) * NPLANE + ppos)

    def plane_peer(d):
        return (3, zpos * NPLANE + (ppos + d) % NPLANE)

    def push(source, target, peer, n):
        pltpu.make_async_remote_copy(
            src_ref=source,
            dst_ref=target,
            send_sem=send_sem.at[n],
            recv_sem=recv_sem.at[n],
            device_id=peer,
            device_id_type=MESH,
        ).start()

    def to_line(source, target, n):
        for d in LINE_FAR:
            push(source, target, line_peer(d), n)

    def to_plane(source, target, n):
        for d in PLANE_FAR:
            push(source, target, plane_peer(d), n)

    def arrived(ref, n):
        pltpu.make_async_copy(ref, ref, recv_sem.at[n]).wait()

    def left_here(ref, n):
        pltpu.make_async_copy(ref, ref, send_sem.at[n]).wait()

    for d in LINE_FAR:
        hello(line_peer(d))

    def keep_post(post, x, slot):
        for n, i in enumerate(EAST):
            east[slot, x + 1, n] = post[i]
        for n, i in enumerate(WEST):
            west[slot, x + 1, n] = post[i]
        for n, i in enumerate(REST):
            rest[slot, x, n] = post[i]

    def streamed(slot, x):
        f = [None] * 19
        for n, i in enumerate(REST):
            if i == 0:
                f[0] = rest[slot, x, 0]
                continue
            source = shifted(rest[slot, x, n], i)
            f[i] = jnp.where(source >= 0.5 * BIG, rest[slot, x, REST.index(OPP[i])], source)
        for n, i in enumerate(EAST):
            source = shifted(east[slot, x, n], i)
            f[i] = jnp.where(source >= 0.5 * BIG, west[slot, x + 1, WEST.index(OPP[i])], source)
        for n, i in enumerate(WEST):
            source = shifted(west[slot, x + 2, n], i)
            f[i] = jnp.where(source >= 0.5 * BIG, east[slot, x + 1, EAST.index(OPP[i])], source)
        return f

    def keep_speeds(u, kind, x):
        for c in range(3):
            speeds[x, c] = jnp.where(kind == 1, 0.0, u[c])

    def halo(slot):
        go_east = pltpu.make_async_remote_copy(
            src_ref=east.at[slot, CX],
            dst_ref=east.at[slot, 0],
            send_sem=halo_send.at[slot, 0],
            recv_sem=halo_recv.at[slot, 0],
            device_id=east_id,
            device_id_type=MESH,
        )
        go_west = pltpu.make_async_remote_copy(
            src_ref=west.at[slot, 1],
            dst_ref=west.at[slot, CX + 1],
            send_sem=halo_send.at[slot, 1],
            recv_sem=halo_recv.at[slot, 1],
            device_id=west_id,
            device_id_type=MESH,
        )
        return go_east, go_west

    def send_halo(slot):
        go_east, go_west = halo(slot)
        odd = slab % 2 == 1

        @pl.when(jnp.logical_and(has_east, odd))
        def _():
            go_east.start()

        @pl.when(has_west)
        def _():
            go_west.start()

        @pl.when(jnp.logical_and(has_east, jnp.logical_not(odd)))
        def _():
            go_east.start()

    def take_halo(slot):
        go_east, go_west = halo(slot)

        @pl.when(has_west)
        def _():
            go_east.wait_recv()

        @pl.when(has_east)
        def _():
            go_west.wait_recv()

    def first_plane(x):
        post, _ = collide([pop[i, x] for i in range(19)], kind_ref[x])
        keep_post(post, x, 0)

    def middle_plane(slot, x):
        kind = kind_ref[x]
        post, u = collide(streamed(slot, x), kind)
        keep_speeds(u, kind, x)
        keep_post(post, x, slot + 1)

    def last_plane(slot, x):
        kind = kind_ref[x]
        f = streamed(slot, x)
        _, u = moments(f)
        keep_speeds(u, kind, x)
        for i in range(19):
            field[i, x] = jnp.where(kind == 1, pop[i, x], f[i])

    def pair(fn):
        def body(n, c):
            fn(n)
            return c

        lax.fori_loop(0, 2, body, 0)

    @pl.when(channel)
    def _():
        for p in range(NPLANE):
            hello((3, zpos * NPLANE + p))

        @pl.when(has_east)
        def _():
            hello(east_id)

        @pl.when(has_west)
        def _():
            hello(west_id)

        samples[...] = jnp.zeros((STEPS, 8, NZ), jnp.float32)
        early[...] = jnp.zeros((16, NZ), jnp.float32)
        staging_b[...] = jnp.zeros((NPLANE, 16, NZ), jnp.float32)

        @pl.when(position == 0)
        def _():
            east[:, 0] = jnp.full((STEPS, 5, NY, NZ), BIG, jnp.float32)

        @pl.when(position == 383)
        def _():
            west[:, CX + 1] = jnp.full((STEPS, 5, NY, NZ), BIG, jnp.float32)

        loads[0].wait()
        loads[1].wait()
        pair(lambda n: first_plane(3 * n))
        edge = jnp.logical_or(position == 0, position == 383)

        @pl.when(edge)
        def _():
            pl.semaphore_wait(barrier, 15 + 8 + 1)

        @pl.when(jnp.logical_not(edge))
        def _():
            pl.semaphore_wait(barrier, 15 + 8 + 2)

        send_halo(0)
        pair(lambda n: first_plane(1 + n))
        loads[2].wait()
        loads[3].wait()

        def pick(n, c):
            found = jnp.int32(-1)
            for z in range(NLINE):
                row = table[group * 128 + z * NPLANE + ppos]
                found = jnp.where(row == 24 * zpos + n, z, found)
            picks[n] = found
            return c

        lax.fori_loop(0, 24, pick, 0)

        lanes = lax.broadcasted_iota(jnp.int32, (NZ, NZ), 1)
        depth = lax.broadcasted_iota(jnp.int32, (NZ, NZ), 0)
        pick_z = (depth == phase[2] + SUB * (lanes % 32)).astype(jnp.float32)
        lane3 = lax.broadcasted_iota(jnp.int32, (3, NY, NZ), 2)
        row3 = lax.broadcasted_iota(jnp.int32, (3, NY, NZ), 1)
        pick_y = row3 == phase[1] + SUB * (lane3 // 32)

        def sample(step):
            plane = speeds[phase[0]].reshape(3 * NY, NZ)
            along = mm(plane, pick_z, ((1,), (0,))).reshape(3, NY, NZ)
            samples[step, 0:3] = jnp.sum(jnp.where(pick_y, along, 0.0), axis=1)

        def one_step(slot, c):
            pair(lambda n: middle_plane(slot, 1 + n))
            take_halo(slot)
            pair(lambda n: middle_plane(slot, 3 * n))
            send_halo(slot + 1)
            sample(slot)
            return c

        lax.fori_loop(0, STEPS - 1, one_step, 0)

        for s in range(3):
            early[4 * s : 4 * s + 4] = samples[s, 0:4]
        line_a[zpos] = early[...]
        to_line(early, line_a.at[zpos], LINE_A)
        pair(lambda n: last_plane(STEPS - 1, 1 + n))
        take_halo(STEPS - 1)
        pair(lambda n: last_plane(STEPS - 1, 3 * n))
        sample(STEPS - 1)
        line_b[zpos] = samples[3]
        to_line(samples.at[3], line_b.at[zpos], LINE_B)

        stores[0].start()
        arrived(line_a.at[0:15], LINE_A)

        def place_a(n, c):
            z = picks[n]
            staging_a[n] = jnp.where(z >= 0, line_a[jnp.maximum(z, 0)], 0.0)
            return c

        lax.fori_loop(0, 24, place_a, 0)
        for p in range(NPLANE):
            push(
                staging_a.at[3 * p : 3 * p + 3],
                landed_a.at[group * NPLANE + ppos],
                (3, zpos * NPLANE + p),
                ROUTE_A,
            )
        arrived(line_b.at[0:15], LINE_B)

        def place_b(p, c):
            for t in range(3):
                z = picks[3 * p + t]
                block = line_b[jnp.maximum(z, 0)]
                staging_b[p, 4 * t : 4 * t + 4] = jnp.where(z >= 0, block, 0.0)[0:4]
            return c

        lax.fori_loop(0, NPLANE, place_b, 0)
        for p in range(NPLANE):
            push(
                staging_b.at[p],
                landed_b.at[group * NPLANE + ppos],
                (3, zpos * NPLANE + p),
                ROUTE_B,
            )

        def sent(slot, c):
            go_east, go_west = halo(slot)

            @pl.when(has_east)
            def _():
                go_east.wait_send()

            @pl.when(has_west)
            def _():
                go_west.wait_send()

            return c

        lax.fori_loop(0, STEPS, sent, 0)
        left_here(line_a.at[0:15], LINE_A)
        left_here(line_b.at[0:15], LINE_B)
        left_here(staging_a, ROUTE_A)
        left_here(staging_b, ROUTE_B)
        stores[0].wait()

    @pl.when(jnp.logical_not(channel))
    def _():
        for n in range(24):
            hello((n // NPLANE, zpos * NPLANE + n % NPLANE))
        for d in PLANE_FAR:
            hello(plane_peer(d))

        loads[5].wait()
        part = mm(modes[...], modes[...], ((0,), (0,)))
        gpart[...] = jnp.zeros((NLINE, 16, RANK), jnp.float32)
        for n in range(NLINE):
            count = min(16, MODES - 16 * n)
            gpart[n, 0:count, 0:MODES] = part[16 * n : 16 * n + count]
        pl.semaphore_wait(barrier, 15 + 24 + 7)

        slot_a[zpos] = gpart[zpos]
        for d in LINE_FAR:
            push(gpart.at[(zpos + d) % NLINE], slot_a.at[zpos], line_peer(d), GRAM_A)
        arrived(slot_a.at[0:15], GRAM_A)
        rows_a[...] = jnp.sum(slot_a[...], axis=0)
        slot_b[ppos] = rows_a[...]
        to_plane(rows_a, slot_b.at[ppos], GRAM_B)
        arrived(slot_b.at[0:7], GRAM_B)
        rows_b[...] = jnp.sum(slot_b[...], axis=0)
        gram[zpos] = rows_b[...]
        to_line(rows_b, gram.at[zpos], GRAM_D)
        arrived(gram.at[0:15], GRAM_D)
        stores[1].start()

        row, col, eye = square_iota()
        matrix, rs_row, _ = unit_diagonal(gram[...].reshape(RANK, RANK))
        scaled[...] = matrix
        inverse[...] = eye - lower_half(matrix - eye, row, col)

        def newton(n, size):
            here = inverse[...]
            error = mm(mm(here, scaled[...], ((1,), (0,))), here, ((1,), (1,))) - eye
            inverse[...] = here - mm(lower_half(error, row, col), here, ((1,), (0,)))
            return jnp.sum(jnp.sum(error * error, axis=0, keepdims=True), axis=1, keepdims=True)

        size = lax.fori_loop(0, NEWTON, newton, jnp.ones((1, 1), jnp.float32))
        good = jnp.broadcast_to(size < 1e-6, (RANK, RANK))
        factor = jnp.where(good, inverse[...], eye) * rs_row
        inverse[...] = factor * SCALE
        q[...] = mm(modes[...], inverse[:, 0:MODES], ((1,), (1,)))
        stores[2].start()
        loads[4].wait()
        small[...] = jnp.zeros((4, 8, NZ), jnp.float32)
        small[0] = jnp.broadcast_to(size, (8, NZ))
        for k in range(4):
            small[0, k + 1 : k + 2] = jnp.full((1, NZ), 1.0, jnp.float32) * order[k].astype(jnp.float32)

        arrived(landed_a, ROUTE_A)
        total = landed_a[0]
        for n in range(1, 24):
            total = total + landed_a[n]
        where_to = lax.broadcasted_iota(jnp.int32, (16, NZ), 1)
        where_from = lax.broadcasted_iota(jnp.int32, (16, NZ), 0)
        for t in range(3):
            for c in range(3):
                n = 3 * t + c
                put = jnp.logical_and(where_from % 4 == c, where_to == 124 + where_from // 4)
                put = jnp.logical_and(put, where_from < 12).astype(jnp.float32)
                block = pl.ds(128 * n, 128)
                q[block, 128:RANK] = q[block, 128:RANK] + mm(total[t], put, ((0,), (0,)))
        snaps[...] = jnp.zeros((8, ROWS_DEV), jnp.float32)
        for t in range(3):
            for c in range(3):
                n = 3 * t + c
                for s in range(3):
                    snaps[s : s + 1, 128 * n : 128 * n + 128] = total[t, 4 * s + c : 4 * s + c + 1]
        product = mm(snaps[...], q[...], ((1,), (0,)))
        cross_own[0:3] = product[0:3, 0:128]
        cross_own[4:7] = product[0:3, 128:RANK]

        arrived(landed_b, ROUTE_B)
        final = landed_b[0]
        for n in range(1, 24):
            final = final + landed_b[n]
        tall = jnp.concatenate([final, jnp.zeros((NZ - 16, NZ), jnp.float32)], axis=0).T
        lane = lax.broadcasted_iota(jnp.int32, (NZ, NZ), 1)
        low_sum = jnp.zeros((8, NZ), jnp.float32)
        high_sum = jnp.zeros((8, NZ), jnp.float32)
        for t in range(3):
            for c in range(3):
                n = 3 * t + c
                block = pl.ds(128 * n, 128)
                column = jnp.broadcast_to(tall[:, 4 * t + c : 4 * t + c + 1], (NZ, NZ))
                high = jnp.where(lane == NZ - 1, column, q[block, 128:RANK])
                q[block, 128:RANK] = high
                low_sum = low_sum + jnp.sum((column * q[block, 0:128]).reshape(16, 8, NZ), axis=0)
                high_sum = high_sum + jnp.sum((column * high).reshape(16, 8, NZ), axis=0)
        cross_own[3:4] = jnp.sum(low_sum, axis=0, keepdims=True)
        cross_own[7:8] = jnp.sum(high_sum, axis=0, keepdims=True)

        cross_a[zpos] = cross_own[...]
        to_line(cross_own, cross_a.at[zpos], CROSS_A)
        stores[3].start()
        arrived(cross_a.at[0:15], CROSS_A)
        cross_mid[...] = jnp.sum(cross_a[...], axis=0)
        cross_b[ppos] = cross_mid[...]
        to_plane(cross_mid, cross_b.at[ppos], CROSS_B)
        arrived(cross_b.at[0:7], CROSS_B)
        both = jnp.sum(cross_b[...], axis=0)
        small[1] = both
        lines = [jnp.concatenate([both[s : s + 1], both[s + 4 : s + 5]], axis=1) for s in range(4)]
        for k, tail in enumerate(last_columns(lines, lambda k, s: order[k] == s)):
            small[2, k : k + 1] = tail[:, 0:128]
            small[3, k : k + 1] = tail[:, 128:RANK]
        stores[4].start()

        left_here(slot_a.at[0:15], GRAM_A)
        left_here(slot_b.at[0:7], GRAM_B)
        left_here(gram.at[0:15], GRAM_D)
        left_here(cross_a.at[0:15], CROSS_A)
        left_here(cross_b.at[0:7], CROSS_B)
        for n in range(1, 5):
            stores[n].wait()


def second_kernel(
    modes_hbm, field, gram_hbm, q_hbm, small_hbm, lattice, basis, passing, q, small, ends, blank, modes, gram, left, inverse, pivots, sem
):
    group = lax.axis_index("group")

    @pl.when(group < 3)
    def _():
        load = pltpu.make_async_copy(field, passing, sem.at[0])
        load.start()
        q[...] = jnp.zeros((ROWS_DEV, RANK), jnp.float32)
        clear = pltpu.make_async_copy(q, basis, sem.at[1])
        clear.start()
        load.wait()
        store = pltpu.make_async_copy(passing, lattice, sem.at[2])
        store.start()
        store.wait()
        clear.wait()

    @pl.when(group == 3)
    def _():
        load_q = pltpu.make_async_copy(q_hbm, q, sem.at[0])
        load_small = pltpu.make_async_copy(small_hbm, small, sem.at[1])
        load_q.start()
        load_small.start()
        blank[...] = jnp.zeros((CX, NY, NZ), jnp.float32)
        clears = [pltpu.make_async_copy(blank, lattice.at[n], sem.at[4 + n]) for n in range(19)]
        for clear in clears:
            clear.start()
        lane = lax.broadcasted_iota(jnp.int32, (ROWS_DEV, 128), 1)
        load_small.wait()
        load_q.wait()

        @pl.when(jnp.logical_not(small[0, 0, 0] < 1e-6))
        def _():
            load = pltpu.make_async_copy(modes_hbm, modes, sem.at[2])
            load.start()
            load_gram = pltpu.make_async_copy(gram_hbm, gram, sem.at[3])
            load_gram.start()
            load_gram.wait()
            row, col, eye = square_iota()
            matrix, rs_row, diagonal = unit_diagonal(gram[...].reshape(RANK, RANK))
            left[...] = matrix
            inverse[...] = eye
            pivots[...] = jnp.ones((RANK, 128), jnp.float32)

            def eliminate(j, c):
                line = left[pl.ds(j, 1), :]
                mine = inverse[pl.ds(j, 1), :]
                along = lax.broadcasted_iota(jnp.int32, (1, RANK), 1)
                pivot = jnp.sum(jnp.where(along == j, line, 0.0), axis=1, keepdims=True)
                column = jnp.sum(jnp.where(col == j, left[...], 0.0), axis=1, keepdims=True)
                below = lax.broadcasted_iota(jnp.int32, (RANK, 1), 0) > j
                factor = jnp.where(below, column / pivot, 0.0)
                left[...] = left[...] - factor * line
                inverse[...] = inverse[...] - factor * mine
                pivots[pl.ds(j, 1), :] = jnp.broadcast_to(pivot, (1, 128))
                return c

            lax.fori_loop(0, RANK, eliminate, 0)
            inverse[...] = inverse[...] / jnp.sqrt(pivots[:, 0:1]) * rs_row
            raw = jnp.concatenate([small[1, 0:4], small[1, 4:8]], axis=1)
            along = lax.broadcasted_iota(jnp.int32, (4, RANK), 1)
            old = jnp.where(along < MODES, raw * jnp.sqrt(diagonal), 0.0)
            old = jnp.concatenate([old, jnp.zeros((4, RANK), jnp.float32)], axis=0)
            fresh = mm(old, inverse[...], ((1,), (1,)))[0:4]
            fresh = jnp.where(along < MODES, fresh, raw)

            def is_step(k, s):
                return small[0, k + 1 : k + 2, 0:1] == float(s)

            rows = last_columns([fresh[s : s + 1] for s in range(4)], is_step)
            for k in range(4):
                small[2, k : k + 1] = rows[k][:, 0:128]
                small[3, k : k + 1] = rows[k][:, 128:RANK]
            load.wait()
            inverse[...] = inverse[...] * SCALE
            whole = mm(modes[...], inverse[:, 0:MODES], ((1,), (1,)))
            wide = lax.broadcasted_iota(jnp.int32, (ROWS_DEV, RANK), 1)
            q[...] = jnp.where(wide < MODES, whole, q[...])

        first = pltpu.make_async_copy(q.at[:, 0:128], basis.at[:, 0:128], sem.at[0])
        first.start()
        rows = jnp.concatenate([small[2, 0:4], small[3, 0:4]], axis=1)
        rows = jnp.concatenate([jnp.zeros((124, RANK), jnp.float32), rows], axis=0)
        ends[...] = jnp.where(lane < 124, q[:, 128:RANK], mm(q[...], rows, ((1,), (1,))))
        second = pltpu.make_async_copy(ends, basis.at[:, 128:RANK], sem.at[1])
        second.start()
        for clear in clears:
            clear.wait()
        first.wait()
        second.wait()


def local(populations, cell_kind, snapshot_order, sample_phase, slab_map, weighted_modes):
    f32 = jnp.float32
    hbm = pl.BlockSpec(memory_space=pltpu.HBM)
    dma = pltpu.SemaphoreType.DMA

    def buffer(*shape):
        return pltpu.VMEM(shape, f32)

    field, gram, q, small = pl.pallas_call(
        first_kernel,
        out_shape=(
            jax.ShapeDtypeStruct((19, CX, NY, NZ), f32),
            jax.ShapeDtypeStruct((NLINE, 16, RANK), f32),
            jax.ShapeDtypeStruct((ROWS_DEV, RANK), f32),
            jax.ShapeDtypeStruct((4, 8, NZ), f32),
        ),
        in_specs=[hbm] * 6,
        out_specs=(hbm,) * 4,
        scratch_shapes=[
            buffer(19, CX, NY, NZ),
            buffer(NLINE, 16, RANK),
            buffer(ROWS_DEV, RANK),
            buffer(4, 8, NZ),
            buffer(19, CX, NY, NZ),
            pltpu.VMEM((CX, NY, NZ), jnp.int32),
            pltpu.SMEM((3,), jnp.int32),
            pltpu.SMEM((4,), jnp.int32),
            pltpu.SMEM((384,), jnp.int32),
            buffer(ROWS_DEV, MODES),
            buffer(STEPS, CX + 2, 5, NY, NZ),
            buffer(STEPS, CX + 2, 5, NY, NZ),
            buffer(STEPS, CX, 9, NY, NZ),
            buffer(CX, 3, NY, NZ),
            buffer(STEPS, 8, NZ),
            buffer(16, NZ),
            buffer(NLINE, 16, NZ),
            buffer(NLINE, 8, NZ),
            buffer(24, 16, NZ),
            buffer(NPLANE, 16, NZ),
            pltpu.SMEM((24,), jnp.int32),
            buffer(24, 3, 16, NZ),
            buffer(24, 16, NZ),
            buffer(NLINE, 16, RANK),
            buffer(NLINE, 16, RANK),
            buffer(NPLANE, 16, RANK),
            buffer(16, RANK),
            buffer(16, RANK),
            buffer(RANK, RANK),
            buffer(RANK, RANK),
            buffer(8, ROWS_DEV),
            buffer(8, NZ),
            buffer(NLINE, 8, NZ),
            buffer(8, NZ),
            buffer(NPLANE, 8, NZ),
            dma((6,)),
            dma((5,)),
            dma((STEPS, 2)),
            dma((STEPS, 2)),
            dma((9,)),
            dma((9,)),
        ],
        compiler_params=pltpu.CompilerParams(
            collective_id=0, has_side_effects=True, vmem_limit_bytes=ROOM
        ),
    )(populations, cell_kind, sample_phase, snapshot_order, slab_map, weighted_modes)
    return pl.pallas_call(
        second_kernel,
        out_shape=(
            jax.ShapeDtypeStruct((19, CX, NY, NZ), f32),
            jax.ShapeDtypeStruct((ROWS_DEV, RANK), f32),
        ),
        in_specs=[hbm] * 5,
        out_specs=(hbm, hbm),
        scratch_shapes=[
            buffer(19, CX, NY, NZ),
            buffer(ROWS_DEV, RANK),
            buffer(4, 8, NZ),
            buffer(ROWS_DEV, 128),
            buffer(CX, NY, NZ),
            buffer(ROWS_DEV, MODES),
            buffer(NLINE, 16, RANK),
            buffer(RANK, RANK),
            buffer(RANK, RANK),
            buffer(RANK, 128),
            dma((4 + 19,)),
        ],
        compiler_params=pltpu.CompilerParams(vmem_limit_bytes=ROOM),
    )(weighted_modes, field, gram, q, small)


def solution(mesh):
    return jax.shard_map(
        local,
        mesh=mesh,
        in_specs=(
            P(None, ("group", "slab"), None, None),
            P(("group", "slab"), None, None),
            P(),
            P(),
            P(),
            P(("group", "slab"), None),
        ),
        out_specs=(P(None, ("group", "slab"), None, None), P(("group", "slab"), None)),
        check_vma=False,
    )
```

time: 127 us -> 110 us (0.87)
  Pallas kernels: 121 us -> 109 us
  local copies, waits for them, and re-layouts: 5.09 us -> 0 us
    pallas_call x1, Pallas kernels: 50.5 us -> 44.3 us  [local(): pl.pallas_call(second_kernel, out_shape=(jax.ShapeDtypeStruct((19, CX, NY...]
    pallas_call x1, Pallas kernels: 70.4 us -> 64.6 us  [local(): pl.pallas_call(first_kernel, out_shape=(jax.ShapeDtypeStruct((19, CX, NY,...]
    unnamed x14 -> x0, local copies, waits for them, and re-layouts: 5.09 us -> none
where the time goes in v2:
time: 110 us
  Pallas kernels  109 us (99%)
    pallas_call x1, Pallas kernels, local(): pl.pallas_call(first_kernel, out_shape=(jax.ShapeDtypeStruct((19, CX, NY,...  64.6 us
    pallas_call x1, Pallas kernels, local(): pl.pallas_call(second_kernel, out_shape=(jax.ShapeDtypeStruct((19, CX, NY...  44.3 us

profile of v2, /device:TPU:7, one launch (start us, length us, event | category | flops | bytes accessed | tf_op | source)
XLA Modules:
  0.0 109.6 jit_solution(5047396836544173133)
XLA Ops:
  0.6 64.6 %shard_map.77 = (f32[19,4,16,128]{3,2,1,0:T(8,128)}, f32[16,16,256]{2,1,0:T(8,128)}, f32[1152,256]{1,0:T(8,128)}, f32[4,8,128]{2,1,0:T(8,128)}) custom-call(f32[19,4,16,128]{3,2,1,0:T(8,128)} %pop_hbm.1, s32[4,16,128]{2,1,0:T(8,128)} %kind_hbm.1, s32[3]{0:T(128)} %phase_hbm.1, s32[4]{0:T(128)} %order_hbm.1, s32[384]{0:T(512)} %table_hbm.1, f32[1152,252]{1,0:T(8,128)} %modes_hbm.3), custom_call_target="tpu_custom_call" | custom-call | tf_op jit(solution)/shard_map/pallas_call | solution.py:785
  65.3 44.3 %shard_map.78 = (f32[19,4,16,128]{3,2,1,0:T(8,128)}, f32[1152,256]{1,0:T(8,128)}) custom-call(f32[1152,252]{1,0:T(8,128)} %modes_hbm.3, f32[19,4,16,128]{3,2,1,0:T(8,128)} %get-tuple-element.6.field, f32[16,16,256]{2,1,0:T(8,128)} %get-tuple-element.7.gram_hbm, f32[1152,256]{1,0:T(8,128)} %get-tuple-element.8.q_hbm, f32[4,8,128]{2,1,0:T(8,128)} %get-tuple-element.9.small_hbm), custom_call_target="tpu_custom_call" | custom-call | tf_op jit(solution)/shard_map/pallas_call | solution.py:842

commit v3 on v2

--- a/solution.py
+++ b/solution.py
@@ -209,18 +209,24 @@
     speeds,
     samples,
     early,
-    line_a,
-    line_b,
-    staging_a,
-    staging_b,
+    final,
     picks,
     landed_a,
+    landed_c,
     landed_b,
-    gpart,
+    ready_a,
+    ready_c,
+    ready_b,
+    got_a,
+    got_c,
+    got_b,
+    pack,
     slot_a,
+    rows_a,
     slot_b,
-    rows_a,
     rows_b,
+    column,
+    square,
     scaled,
     inverse,
     snaps,
@@ -245,7 +251,8 @@
     has_east = jnp.logical_and(channel, position < 383)
     west_id = ((position - 1) // 128, (position + 127) % 128)
     east_id = ((position + 1) // 128, (position + 1) % 128)
-    LINE_A, LINE_B, ROUTE_A, ROUTE_B, GRAM_A, GRAM_B, GRAM_D, CROSS_A, CROSS_B = range(9)
+    ROUTE_A, ROUTE_C, ROUTE_B, LINE_A, LINE_C, LINE_B, GRAM_A, GRAM_B, GRAM_C, GRAM_D, CROSS_A, CROSS_B = range(12)
+    odd = slab % 2
 
     barrier = pltpu.get_barrier_semaphore()
 
@@ -271,7 +278,7 @@
         for n, (a, b) in enumerate(
             [
                 (field, field_hbm),
-                (gram, gram_hbm),
+                (square, gram_hbm),
                 (q.at[:, 0:128], q_hbm.at[:, 0:128]),
                 (q.at[:, 128:RANK], q_hbm.at[:, 128:RANK]),
                 (small, small_hbm),
@@ -281,13 +288,14 @@
 
     @pl.when(channel)
     def _():
-        for n in range(4):
+        for n in range(3):
             loads[n].start()
 
     @pl.when(jnp.logical_not(channel))
     def _():
         loads[5].start()
         loads[4].start()
+        loads[3].start()
 
     def line_peer(d):
         return (group, ((zpos + d) % NLINE) * NPLANE + ppos)
@@ -318,9 +326,6 @@
 
     def left_here(ref, n):
         pltpu.make_async_copy(ref, ref, send_sem.at[n]).wait()
-
-    for d in LINE_FAR:
-        hello(line_peer(d))
 
     def keep_post(post, x, slot):
         for n, i in enumerate(EAST):
@@ -369,32 +374,34 @@
         )
         return go_east, go_west
 
-    def send_halo(slot):
+    def send_side(slot, side):
         go_east, go_west = halo(slot)
-        odd = slab % 2 == 1
-
-        @pl.when(jnp.logical_and(has_east, odd))
+
+        @pl.when(jnp.logical_and(has_east, side == 1))
         def _():
             go_east.start()
 
-        @pl.when(has_west)
+        @pl.when(jnp.logical_and(has_west, side == 0))
         def _():
             go_west.start()
 
-        @pl.when(jnp.logical_and(has_east, jnp.logical_not(odd)))
-        def _():
-            go_east.start()
-
-    def take_halo(slot):
+    def take_side(slot, side):
         go_east, go_west = halo(slot)
 
-        @pl.when(has_west)
+        @pl.when(jnp.logical_and(has_east, side == 1))
+        def _():
+            go_west.wait_recv()
+
+        @pl.when(jnp.logical_and(has_west, side == 0))
         def _():
             go_east.wait_recv()
 
-        @pl.when(has_east)
-        def _():
-            go_west.wait_recv()
+    def sides(fn):
+        def body(n, c):
+            fn((odd + n) % 2)
+            return c
+
+        lax.fori_loop(0, 2, body, 0)
 
     def first_plane(x):
         post, _ = collide([pop[i, x] for i in range(19)], kind_ref[x])
@@ -423,9 +430,6 @@
 
     @pl.when(channel)
     def _():
-        for p in range(NPLANE):
-            hello((3, zpos * NPLANE + p))
-
         @pl.when(has_east)
         def _():
             hello(east_id)
@@ -434,9 +438,7 @@
         def _():
             hello(west_id)
 
-        samples[...] = jnp.zeros((STEPS, 8, NZ), jnp.float32)
-        early[...] = jnp.zeros((16, NZ), jnp.float32)
-        staging_b[...] = jnp.zeros((NPLANE, 16, NZ), jnp.float32)
+        samples[...] = jnp.zeros((STEPS, 4, NZ), jnp.float32)
 
         @pl.when(position == 0)
         def _():
@@ -448,31 +450,20 @@
 
         loads[0].wait()
         loads[1].wait()
-        pair(lambda n: first_plane(3 * n))
+        sides(lambda side: first_plane(3 * side))
         edge = jnp.logical_or(position == 0, position == 383)
 
         @pl.when(edge)
         def _():
-            pl.semaphore_wait(barrier, 15 + 8 + 1)
+            pl.semaphore_wait(barrier, 8 + 1)
 
         @pl.when(jnp.logical_not(edge))
         def _():
-            pl.semaphore_wait(barrier, 15 + 8 + 2)
-
-        send_halo(0)
+            pl.semaphore_wait(barrier, 8 + 2)
+
+        sides(lambda side: send_side(0, side))
         pair(lambda n: first_plane(1 + n))
         loads[2].wait()
-        loads[3].wait()
-
-        def pick(n, c):
-            found = jnp.int32(-1)
-            for z in range(NLINE):
-                row = table[group * 128 + z * NPLANE + ppos]
-                found = jnp.where(row == 24 * zpos + n, z, found)
-            picks[n] = found
-            return c
-
-        lax.fori_loop(0, 24, pick, 0)
 
         lanes = lax.broadcasted_iota(jnp.int32, (NZ, NZ), 1)
         depth = lax.broadcasted_iota(jnp.int32, (NZ, NZ), 0)
@@ -486,60 +477,36 @@
             along = mm(plane, pick_z, ((1,), (0,))).reshape(3, NY, NZ)
             samples[step, 0:3] = jnp.sum(jnp.where(pick_y, along, 0.0), axis=1)
 
+        def to_analysis(source, target, n):
+            for d in [4, 5, 3, 6, 2, 7, 1, 0]:
+                push(source, target.at[group * NPLANE + ppos], (3, zpos * NPLANE + (ppos + d) % NPLANE), n)
+
         def one_step(slot, c):
             pair(lambda n: middle_plane(slot, 1 + n))
-            take_halo(slot)
-            pair(lambda n: middle_plane(slot, 3 * n))
-            send_halo(slot + 1)
+
+            def one_side(side):
+                take_side(slot, side)
+                middle_plane(slot, 3 * side)
+                send_side(slot + 1, side)
+
+            sides(one_side)
             sample(slot)
             return c
 
-        lax.fori_loop(0, STEPS - 1, one_step, 0)
-
-        for s in range(3):
-            early[4 * s : 4 * s + 4] = samples[s, 0:4]
-        line_a[zpos] = early[...]
-        to_line(early, line_a.at[zpos], LINE_A)
+        lax.fori_loop(0, 2, one_step, 0)
+        to_analysis(samples.at[0:2], landed_a, ROUTE_A)
+        one_step(2, 0)
+        to_analysis(samples.at[2], landed_c, ROUTE_C)
         pair(lambda n: last_plane(STEPS - 1, 1 + n))
-        take_halo(STEPS - 1)
-        pair(lambda n: last_plane(STEPS - 1, 3 * n))
+
+        def last_side(side):
+            take_side(STEPS - 1, side)
+            last_plane(STEPS - 1, 3 * side)
+
+        sides(last_side)
         sample(STEPS - 1)
-        line_b[zpos] = samples[3]
-        to_line(samples.at[3], line_b.at[zpos], LINE_B)
-
+        to_analysis(samples.at[3], landed_b, ROUTE_B)
         stores[0].start()
-        arrived(line_a.at[0:15], LINE_A)
-
-        def place_a(n, c):
-            z = picks[n]
-            staging_a[n] = jnp.where(z >= 0, line_a[jnp.maximum(z, 0)], 0.0)
-            return c
-
-        lax.fori_loop(0, 24, place_a, 0)
-        for p in range(NPLANE):
-            push(
-                staging_a.at[3 * p : 3 * p + 3],
-                landed_a.at[group * NPLANE + ppos],
-                (3, zpos * NPLANE + p),
-                ROUTE_A,
-            )
-        arrived(line_b.at[0:15], LINE_B)
-
-        def place_b(p, c):
-            for t in range(3):
-                z = picks[3 * p + t]
-                block = line_b[jnp.maximum(z, 0)]
-                staging_b[p, 4 * t : 4 * t + 4] = jnp.where(z >= 0, block, 0.0)[0:4]
-            return c
-
-        lax.fori_loop(0, NPLANE, place_b, 0)
-        for p in range(NPLANE):
-            push(
-                staging_b.at[p],
-                landed_b.at[group * NPLANE + ppos],
-                (3, zpos * NPLANE + p),
-                ROUTE_B,
-            )
 
         def sent(slot, c):
             go_east, go_west = halo(slot)
@@ -555,43 +522,84 @@
             return c
 
         lax.fori_loop(0, STEPS, sent, 0)
-        left_here(line_a.at[0:15], LINE_A)
-        left_here(line_b.at[0:15], LINE_B)
-        left_here(staging_a, ROUTE_A)
-        left_here(staging_b, ROUTE_B)
+        left_here(landed_a.at[0:8], ROUTE_A)
+        left_here(landed_c.at[0:8], ROUTE_C)
+        left_here(landed_b.at[0:8], ROUTE_B)
         stores[0].wait()
 
     @pl.when(jnp.logical_not(channel))
     def _():
         for n in range(24):
             hello((n // NPLANE, zpos * NPLANE + n % NPLANE))
+        for d in LINE_FAR:
+            hello(line_peer(d))
         for d in PLANE_FAR:
             hello(plane_peer(d))
 
+        square[...] = jnp.zeros((RANK, RANK), jnp.float32)
         loads[5].wait()
-        part = mm(modes[...], modes[...], ((0,), (0,)))
-        gpart[...] = jnp.zeros((NLINE, 16, RANK), jnp.float32)
-        for n in range(NLINE):
-            count = min(16, MODES - 16 * n)
-            gpart[n, 0:count, 0:MODES] = part[16 * n : 16 * n + count]
-        pl.semaphore_wait(barrier, 15 + 24 + 7)
-
-        slot_a[zpos] = gpart[zpos]
+        square[0:MODES, 0:MODES] = mm(modes[...], modes[...], ((0,), (0,)))
+        for p in range(NPLANE):
+            for z in range(NLINE):
+                down, across = 32 * p + 4 * (z // 2), 128 * (z % 2)
+                pack[p, z] = square[down : down + 4, across : across + 128]
+        pl.semaphore_wait(barrier, 15 + 7)
+
+        slot_a[ppos] = pack[ppos]
+        for d in PLANE_FAR:
+            push(pack.at[(ppos + d) % NPLANE], slot_a.at[ppos], plane_peer(d), GRAM_A)
+
+        loads[3].wait()
+
+        def pick(n, c):
+            found = jnp.int32(-1)
+            wanted = 24 * (n // 3) + 3 * ppos + n % 3
+            for g in range(3):
+                for p in range(NPLANE):
+                    row = table[g * 128 + zpos * NPLANE + p]
+                    found = jnp.where(row == wanted, g * NPLANE + p, found)
+            picks[n] = found
+            return c
+
+        lax.fori_loop(0, 48, pick, 0)
+
+        def forward(landed, ready, got, from_sem, to_sem):
+            arrived(landed, from_sem)
+
+            def place(n, c):
+                source = picks[n]
+                ready[n] = jnp.where(source >= 0, landed[jnp.maximum(source, 0)], 0.0)
+                return c
+
+            lax.fori_loop(0, 48, place, 0)
+            got[zpos] = ready[pl.ds(3 * zpos, 3)]
+            for d in LINE_FAR:
+                push(ready.at[pl.ds(3 * ((zpos + d) % NLINE), 3)], got.at[zpos], line_peer(d), to_sem)
+
+        arrived(slot_a.at[0:7], GRAM_A)
+        rows_a[...] = jnp.sum(slot_a[...], axis=0)
+        slot_b[zpos] = rows_a[zpos]
         for d in LINE_FAR:
-            push(gpart.at[(zpos + d) % NLINE], slot_a.at[zpos], line_peer(d), GRAM_A)
-        arrived(slot_a.at[0:15], GRAM_A)
-        rows_a[...] = jnp.sum(slot_a[...], axis=0)
-        slot_b[ppos] = rows_a[...]
-        to_plane(rows_a, slot_b.at[ppos], GRAM_B)
-        arrived(slot_b.at[0:7], GRAM_B)
+            push(rows_a.at[(zpos + d) % NLINE], slot_b.at[zpos], line_peer(d), GRAM_B)
+        arrived(slot_b.at[0:15], GRAM_B)
         rows_b[...] = jnp.sum(slot_b[...], axis=0)
-        gram[zpos] = rows_b[...]
-        to_line(rows_b, gram.at[zpos], GRAM_D)
-        arrived(gram.at[0:15], GRAM_D)
+        column[zpos] = rows_b[...]
+        to_line(rows_b, column.at[zpos], GRAM_C)
+        forward(landed_a, ready_a, got_a, ROUTE_A, LINE_A)
+        arrived(column.at[0:15], GRAM_C)
+        gram[ppos] = column[...]
+        to_plane(column, gram.at[ppos], GRAM_D)
+        forward(landed_c, ready_c, got_c, ROUTE_C, LINE_C)
+        arrived(gram.at[0:7], GRAM_D)
+        forward(landed_b, ready_b, got_b, ROUTE_B, LINE_B)
+        for p in range(NPLANE):
+            for z in range(NLINE):
+                down, across = 32 * p + 4 * (z // 2), 128 * (z % 2)
+                square[down : down + 4, across : across + 128] = gram[p, z]
         stores[1].start()
 
         row, col, eye = square_iota()
-        matrix, rs_row, _ = unit_diagonal(gram[...].reshape(RANK, RANK))
+        matrix, rs_row, _ = unit_diagonal(square[...])
         scaled[...] = matrix
         inverse[...] = eye - lower_half(matrix - eye, row, col)
 
@@ -613,10 +621,15 @@
         for k in range(4):
             small[0, k + 1 : k + 2] = jnp.full((1, NZ), 1.0, jnp.float32) * order[k].astype(jnp.float32)
 
-        arrived(landed_a, ROUTE_A)
-        total = landed_a[0]
-        for n in range(1, 24):
-            total = total + landed_a[n]
+        arrived(got_a.at[0:15], LINE_A)
+        arrived(got_c.at[0:15], LINE_C)
+        sum_a = jnp.sum(got_a[...], axis=0)
+        sum_c = jnp.sum(got_c[...], axis=0)
+        early[...] = jnp.zeros((3, 16, NZ), jnp.float32)
+        for t in range(3):
+            early[t, 0:4] = sum_a[t, 0]
+            early[t, 4:8] = sum_a[t, 1]
+            early[t, 8:12] = sum_c[t]
         where_to = lax.broadcasted_iota(jnp.int32, (16, NZ), 1)
         where_from = lax.broadcasted_iota(jnp.int32, (16, NZ), 0)
         for t in range(3):
@@ -625,22 +638,23 @@
                 put = jnp.logical_and(where_from % 4 == c, where_to == 124 + where_from // 4)
                 put = jnp.logical_and(put, where_from < 12).astype(jnp.float32)
                 block = pl.ds(128 * n, 128)
-                q[block, 128:RANK] = q[block, 128:RANK] + mm(total[t], put, ((0,), (0,)))
+                q[block, 128:RANK] = q[block, 128:RANK] + mm(early[t], put, ((0,), (0,)))
         snaps[...] = jnp.zeros((8, ROWS_DEV), jnp.float32)
         for t in range(3):
             for c in range(3):
                 n = 3 * t + c
                 for s in range(3):
-                    snaps[s : s + 1, 128 * n : 128 * n + 128] = total[t, 4 * s + c : 4 * s + c + 1]
+                    snaps[s : s + 1, 128 * n : 128 * n + 128] = early[t, 4 * s + c : 4 * s + c + 1]
         product = mm(snaps[...], q[...], ((1,), (0,)))
         cross_own[0:3] = product[0:3, 0:128]
         cross_own[4:7] = product[0:3, 128:RANK]
 
-        arrived(landed_b, ROUTE_B)
-        final = landed_b[0]
-        for n in range(1, 24):
-            final = final + landed_b[n]
-        tall = jnp.concatenate([final, jnp.zeros((NZ - 16, NZ), jnp.float32)], axis=0).T
+        arrived(got_b.at[0:15], LINE_B)
+        sum_b = jnp.sum(got_b[...], axis=0)
+        final[...] = jnp.zeros((NZ, NZ), jnp.float32)
+        for t in range(3):
+            final[4 * t : 4 * t + 4] = sum_b[t]
+        tall = final[...].T
         lane = lax.broadcasted_iota(jnp.int32, (NZ, NZ), 1)
         low_sum = jnp.zeros((8, NZ), jnp.float32)
         high_sum = jnp.zeros((8, NZ), jnp.float32)
@@ -648,11 +662,11 @@
             for c in range(3):
                 n = 3 * t + c
                 block = pl.ds(128 * n, 128)
-                column = jnp.broadcast_to(tall[:, 4 * t + c : 4 * t + c + 1], (NZ, NZ))
-                high = jnp.where(lane == NZ - 1, column, q[block, 128:RANK])
+                wide = jnp.broadcast_to(tall[:, 4 * t + c : 4 * t + c + 1], (NZ, NZ))
+                high = jnp.where(lane == NZ - 1, wide, q[block, 128:RANK])
                 q[block, 128:RANK] = high
-                low_sum = low_sum + jnp.sum((column * q[block, 0:128]).reshape(16, 8, NZ), axis=0)
-                high_sum = high_sum + jnp.sum((column * high).reshape(16, 8, NZ), axis=0)
+                low_sum = low_sum + jnp.sum((wide * q[block, 0:128]).reshape(16, 8, NZ), axis=0)
+                high_sum = high_sum + jnp.sum((wide * high).reshape(16, 8, NZ), axis=0)
         cross_own[3:4] = jnp.sum(low_sum, axis=0, keepdims=True)
         cross_own[7:8] = jnp.sum(high_sum, axis=0, keepdims=True)
 
@@ -672,9 +686,13 @@
             small[3, k : k + 1] = tail[:, 128:RANK]
         stores[4].start()
 
-        left_here(slot_a.at[0:15], GRAM_A)
-        left_here(slot_b.at[0:7], GRAM_B)
-        left_here(gram.at[0:15], GRAM_D)
+        left_here(slot_a.at[0:7], GRAM_A)
+        left_here(slot_b.at[0:15], GRAM_B)
+        left_here(column.at[0:15], GRAM_C)
+        left_here(gram.at[0:7], GRAM_D)
+        left_here(got_a.at[0:15], LINE_A)
+        left_here(got_c.at[0:15], LINE_C)
+        left_here(got_b.at[0:15], LINE_B)
         left_here(cross_a.at[0:15], CROSS_A)
         left_here(cross_b.at[0:7], CROSS_B)
         for n in range(1, 5):
@@ -721,7 +739,7 @@
             load_gram.start()
             load_gram.wait()
             row, col, eye = square_iota()
-            matrix, rs_row, diagonal = unit_diagonal(gram[...].reshape(RANK, RANK))
+            matrix, rs_row, diagonal = unit_diagonal(gram[...])
             left[...] = matrix
             inverse[...] = eye
             pivots[...] = jnp.ones((RANK, 128), jnp.float32)
@@ -786,7 +804,7 @@
         first_kernel,
         out_shape=(
             jax.ShapeDtypeStruct((19, CX, NY, NZ), f32),
-            jax.ShapeDtypeStruct((NLINE, 16, RANK), f32),
+            jax.ShapeDtypeStruct((RANK, RANK), f32),
             jax.ShapeDtypeStruct((ROWS_DEV, RANK), f32),
             jax.ShapeDtypeStruct((4, 8, NZ), f32),
         ),
@@ -794,7 +812,7 @@
         out_specs=(hbm,) * 4,
         scratch_shapes=[
             buffer(19, CX, NY, NZ),
-            buffer(NLINE, 16, RANK),
+            buffer(NPLANE, NLINE, 4, NZ),
             buffer(ROWS_DEV, RANK),
             buffer(4, 8, NZ),
             buffer(19, CX, NY, NZ),
@@ -807,20 +825,26 @@
             buffer(STEPS, CX + 2, 5, NY, NZ),
             buffer(STEPS, CX, 9, NY, NZ),
             buffer(CX, 3, NY, NZ),
-            buffer(STEPS, 8, NZ),
-            buffer(16, NZ),
-            buffer(NLINE, 16, NZ),
-            buffer(NLINE, 8, NZ),
-            buffer(24, 16, NZ),
-            buffer(NPLANE, 16, NZ),
-            pltpu.SMEM((24,), jnp.int32),
-            buffer(24, 3, 16, NZ),
-            buffer(24, 16, NZ),
-            buffer(NLINE, 16, RANK),
-            buffer(NLINE, 16, RANK),
-            buffer(NPLANE, 16, RANK),
-            buffer(16, RANK),
-            buffer(16, RANK),
+            buffer(STEPS, 4, NZ),
+            buffer(3, 16, NZ),
+            buffer(NZ, NZ),
+            pltpu.SMEM((48,), jnp.int32),
+            buffer(24, 2, 4, NZ),
+            buffer(24, 4, NZ),
+            buffer(24, 4, NZ),
+            buffer(48, 2, 4, NZ),
+            buffer(48, 4, NZ),
+            buffer(48, 4, NZ),
+            buffer(NLINE, 3, 2, 4, NZ),
+            buffer(NLINE, 3, 4, NZ),
+            buffer(NLINE, 3, 4, NZ),
+            buffer(NPLANE, NLINE, 4, NZ),
+            buffer(NPLANE, NLINE, 4, NZ),
+            buffer(NLINE, 4, NZ),
+            buffer(NLINE, 4, NZ),
+            buffer(4, NZ),
+            buffer(NLINE, 4, NZ),
+            buffer(RANK, RANK),
             buffer(RANK, RANK),
             buffer(RANK, RANK),
             buffer(8, ROWS_DEV),
@@ -832,8 +856,8 @@
             dma((5,)),
             dma((STEPS, 2)),
             dma((STEPS, 2)),
-            dma((9,)),
-            dma((9,)),
+            dma((12,)),
+            dma((12,)),
         ],
         compiler_params=pltpu.CompilerParams(
             collective_id=0, has_side_effects=True, vmem_limit_bytes=ROOM
@@ -854,7 +878,7 @@
             buffer(ROWS_DEV, 128),
             buffer(CX, NY, NZ),
             buffer(ROWS_DEV, MODES),
-            buffer(NLINE, 16, RANK),
+            buffer(RANK, RANK),
             buffer(RANK, RANK),
             buffer(RANK, RANK),
             buffer(RANK, 128),

time: 110 us -> 104 us (0.945)
  Pallas kernels: 109 us -> 103 us
    pallas_call x1, Pallas kernels: 64.6 us -> 58.6 us  [local(): pl.pallas_call(first_kernel, out_shape=(jax.ShapeDtypeStruct((19, CX, NY,...]
where the time goes in v3:
time: 104 us
  Pallas kernels  103 us (99%)
    pallas_call x1, Pallas kernels, local(): pl.pallas_call(first_kernel, out_shape=(jax.ShapeDtypeStruct((19, CX, NY,...  58.6 us
    pallas_call x1, Pallas kernels, local(): pl.pallas_call(second_kernel, out_shape=(jax.ShapeDtypeStruct((19, CX, NY...  44.3 us

profile of v3, /device:TPU:7, one launch (start us, length us, event | category | flops | bytes accessed | tf_op | source)
XLA Modules:
  0.0 103.6 jit_solution(17730511773694904423)
XLA Ops:
  0.6 58.6 %shard_map.77 = (f32[19,4,16,128]{3,2,1,0:T(8,128)}, f32[256,256]{1,0:T(8,128)}, f32[1152,256]{1,0:T(8,128)}, f32[4,8,128]{2,1,0:T(8,128)}) custom-call(f32[19,4,16,128]{3,2,1,0:T(8,128)} %pop_hbm.1, s32[4,16,128]{2,1,0:T(8,128)} %kind_hbm.1, s32[3]{0:T(128)} %phase_hbm.1, s32[4]{0:T(128)} %order_hbm.1, s32[384]{0:T(512)} %table_hbm.1, f32[1152,252]{1,0:T(8,128)} %modes_hbm.3), custom_call_target="tpu_custom_call" | custom-call | tf_op jit(solution)/shard_map/pallas_call | solution.py:803
  59.3 44.3 %shard_map.78 = (f32[19,4,16,128]{3,2,1,0:T(8,128)}, f32[1152,256]{1,0:T(8,128)}) custom-call(f32[1152,252]{1,0:T(8,128)} %modes_hbm.3, f32[19,4,16,128]{3,2,1,0:T(8,128)} %get-tuple-element.6.field, f32[256,256]{1,0:T(8,128)} %get-tuple-element.7.gram_hbm, f32[1152,256]{1,0:T(8,128)} %get-tuple-element.8.q_hbm, f32[4,8,128]{2,1,0:T(8,128)} %get-tuple-element.9.small_hbm), custom_call_target="tpu_custom_call" | custom-call | tf_op jit(solution)/shard_map/pallas_call | solution.py:866

commit v4 on v3

--- a/solution.py
+++ b/solution.py
@@ -50,10 +50,11 @@
 ROWS_DEV = 1152
 ROWS_ALL = 128 * ROWS_DEV
 SCALE = math.sqrt(ROWS_ALL)
-NEWTON = 3
+NEWTON = 2
 ROOM = 60 * 1024 * 1024
 LINE_FAR = [8, 7, 9, 6, 10, 5, 11, 4, 12, 3, 13, 2, 14, 1, 15]
 PLANE_FAR = [4, 5, 3, 6, 2, 7, 1]
+FAR_ALL = PLANE_FAR + [0]
 
 
 def mm(a, b, dims):
@@ -168,17 +169,21 @@
     for s in range(4):
         start.append(SCALE * (lane == MODES + s).astype(jnp.float32) - old[s] * (SCALE / ROWS_ALL))
     low = [[None] * 4 for _ in range(4)]
+    over = [None] * 4
     result = []
     for k in range(4):
         for j in range(k + 1):
             value = entry[k][j]
             for m in range(j):
                 value = value - low[k][m] * low[j][m]
-            low[k][j] = jnp.sqrt(value) if k == j else value / low[j][j]
+            if k == j:
+                over[k] = 1.0 / jnp.sqrt(value)
+            else:
+                low[k][j] = value * over[j]
         line = chosen(k, start)
         for m in range(k):
             line = line - low[k][m] * result[m]
-        result.append(line / low[k][k])
+        result.append(line * over[k])
     return result
 
 
@@ -230,6 +235,7 @@
     scaled,
     inverse,
     snaps,
+    tails,
     cross_own,
     cross_a,
     cross_mid,
@@ -240,6 +246,7 @@
     halo_recv,
     send_sem,
     recv_sem,
+    go_sem,
 ):
     group = lax.axis_index("group")
     slab = lax.axis_index("slab")
@@ -263,12 +270,14 @@
         pltpu.make_async_copy(a, b, load_sem.at[n])
         for n, (a, b) in enumerate(
             [
-                (pop_hbm, pop),
+                (pop_hbm.at[:, 0], pop.at[:, 0]),
                 (kind_hbm, kind_ref),
                 (phase_hbm, phase),
                 (table_hbm, table),
                 (order_hbm, order),
                 (modes_hbm, modes),
+                (pop_hbm.at[:, CX - 1], pop.at[:, CX - 1]),
+                (pop_hbm.at[:, 1 : CX - 1], pop.at[:, 1 : CX - 1]),
             ]
         )
     ]
@@ -288,7 +297,7 @@
 
     @pl.when(channel)
     def _():
-        for n in range(3):
+        for n in (0, 6, 1, 7, 2):
             loads[n].start()
 
     @pl.when(jnp.logical_not(channel))
@@ -438,6 +447,9 @@
         def _():
             hello(west_id)
 
+        for d in FAR_ALL:
+            hello((3, zpos * NPLANE + (ppos + d) % NPLANE))
+
         samples[...] = jnp.zeros((STEPS, 4, NZ), jnp.float32)
 
         @pl.when(position == 0)
@@ -448,20 +460,21 @@
         def _():
             west[:, CX + 1] = jnp.full((STEPS, 5, NY, NZ), BIG, jnp.float32)
 
-        loads[0].wait()
-        loads[1].wait()
+        for n in (0, 6, 1):
+            loads[n].wait()
         sides(lambda side: first_plane(3 * side))
         edge = jnp.logical_or(position == 0, position == 383)
 
         @pl.when(edge)
         def _():
-            pl.semaphore_wait(barrier, 8 + 1)
+            pl.semaphore_wait(barrier, 1)
 
         @pl.when(jnp.logical_not(edge))
         def _():
-            pl.semaphore_wait(barrier, 8 + 2)
+            pl.semaphore_wait(barrier, 2)
 
         sides(lambda side: send_side(0, side))
+        loads[7].wait()
         pair(lambda n: first_plane(1 + n))
         loads[2].wait()
 
@@ -478,7 +491,7 @@
             samples[step, 0:3] = jnp.sum(jnp.where(pick_y, along, 0.0), axis=1)
 
         def to_analysis(source, target, n):
-            for d in [4, 5, 3, 6, 2, 7, 1, 0]:
+            for d in FAR_ALL:
                 push(source, target.at[group * NPLANE + ppos], (3, zpos * NPLANE + (ppos + d) % NPLANE), n)
 
         def one_step(slot, c):
@@ -494,6 +507,7 @@
             return c
 
         lax.fori_loop(0, 2, one_step, 0)
+        pl.semaphore_wait(go_sem, 8)
         to_analysis(samples.at[0:2], landed_a, ROUTE_A)
         one_step(2, 0)
         to_analysis(samples.at[2], landed_c, ROUTE_C)
@@ -529,8 +543,6 @@
 
     @pl.when(jnp.logical_not(channel))
     def _():
-        for n in range(24):
-            hello((n // NPLANE, zpos * NPLANE + n % NPLANE))
         for d in LINE_FAR:
             hello(line_peer(d))
         for d in PLANE_FAR:
@@ -543,11 +555,19 @@
             for z in range(NLINE):
                 down, across = 32 * p + 4 * (z // 2), 128 * (z % 2)
                 pack[p, z] = square[down : down + 4, across : across + 128]
-        pl.semaphore_wait(barrier, 15 + 7)
+        pl.semaphore_wait(barrier, 15 + 7 + 24)
 
         slot_a[ppos] = pack[ppos]
         for d in PLANE_FAR:
             push(pack.at[(ppos + d) % NPLANE], slot_a.at[ppos], plane_peer(d), GRAM_A)
+
+        for n in range(24):
+            pl.semaphore_signal(
+                go_sem,
+                inc=1,
+                device_id=(n // NPLANE, zpos * NPLANE + (ppos + n) % NPLANE),
+                device_id_type=MESH,
+            )
 
         loads[3].wait()
 
@@ -598,29 +618,6 @@
                 square[down : down + 4, across : across + 128] = gram[p, z]
         stores[1].start()
 
-        row, col, eye = square_iota()
-        matrix, rs_row, _ = unit_diagonal(square[...])
-        scaled[...] = matrix
-        inverse[...] = eye - lower_half(matrix - eye, row, col)
-
-        def newton(n, size):
-            here = inverse[...]
-            error = mm(mm(here, scaled[...], ((1,), (0,))), here, ((1,), (1,))) - eye
-            inverse[...] = here - mm(lower_half(error, row, col), here, ((1,), (0,)))
-            return jnp.sum(jnp.sum(error * error, axis=0, keepdims=True), axis=1, keepdims=True)
-
-        size = lax.fori_loop(0, NEWTON, newton, jnp.ones((1, 1), jnp.float32))
-        good = jnp.broadcast_to(size < 1e-6, (RANK, RANK))
-        factor = jnp.where(good, inverse[...], eye) * rs_row
-        inverse[...] = factor * SCALE
-        q[...] = mm(modes[...], inverse[:, 0:MODES], ((1,), (1,)))
-        stores[2].start()
-        loads[4].wait()
-        small[...] = jnp.zeros((4, 8, NZ), jnp.float32)
-        small[0] = jnp.broadcast_to(size, (8, NZ))
-        for k in range(4):
-            small[0, k + 1 : k + 2] = jnp.full((1, NZ), 1.0, jnp.float32) * order[k].astype(jnp.float32)
-
         arrived(got_a.at[0:15], LINE_A)
         arrived(got_c.at[0:15], LINE_C)
         sum_a = jnp.sum(got_a[...], axis=0)
@@ -638,13 +635,39 @@
                 put = jnp.logical_and(where_from % 4 == c, where_to == 124 + where_from // 4)
                 put = jnp.logical_and(put, where_from < 12).astype(jnp.float32)
                 block = pl.ds(128 * n, 128)
-                q[block, 128:RANK] = q[block, 128:RANK] + mm(early[t], put, ((0,), (0,)))
+                tails[block, :] = mm(early[t], put, ((0,), (0,)))
         snaps[...] = jnp.zeros((8, ROWS_DEV), jnp.float32)
         for t in range(3):
             for c in range(3):
                 n = 3 * t + c
                 for s in range(3):
                     snaps[s : s + 1, 128 * n : 128 * n + 128] = early[t, 4 * s + c : 4 * s + c + 1]
+
+        row, col, eye = square_iota()
+        matrix, rs_row, _ = unit_diagonal(square[...])
+        scaled[...] = matrix
+        inverse[...] = eye - lower_half(matrix - eye, row, col)
+
+        def newton(n, size):
+            here = inverse[...]
+            error = mm(mm(here, scaled[...], ((1,), (0,))), here, ((1,), (1,))) - eye
+            inverse[...] = here - mm(lower_half(error, row, col), here, ((1,), (0,)))
+            return jnp.sum(jnp.sum(error * error, axis=0, keepdims=True), axis=1, keepdims=True)
+
+        size = lax.fori_loop(0, NEWTON, newton, jnp.ones((1, 1), jnp.float32))
+        good = jnp.broadcast_to(size < 1e-6, (RANK, RANK))
+        factor = jnp.where(good, inverse[...], eye) * rs_row
+        inverse[...] = factor * SCALE
+        projected = mm(modes[...], inverse[:, 0:MODES], ((1,), (1,)))
+        q[:, 0:128] = projected[:, 0:128]
+        q[:, 128:RANK] = projected[:, 128:RANK] + tails[...]
+        stores[2].start()
+        loads[4].wait()
+        small[...] = jnp.zeros((4, 8, NZ), jnp.float32)
+        small[0] = jnp.broadcast_to(size, (8, NZ))
+        for k in range(4):
+            small[0, k + 1 : k + 2] = jnp.full((1, NZ), 1.0, jnp.float32) * order[k].astype(jnp.float32)
+
         product = mm(snaps[...], q[...], ((1,), (0,)))
         cross_own[0:3] = product[0:3, 0:128]
         cross_own[4:7] = product[0:3, 128:RANK]
@@ -848,16 +871,18 @@
             buffer(RANK, RANK),
             buffer(RANK, RANK),
             buffer(8, ROWS_DEV),
+            buffer(ROWS_DEV, 128),
             buffer(8, NZ),
             buffer(NLINE, 8, NZ),
             buffer(8, NZ),
             buffer(NPLANE, 8, NZ),
-            dma((6,)),
+            dma((8,)),
             dma((5,)),
             dma((STEPS, 2)),
             dma((STEPS, 2)),
             dma((12,)),
             dma((12,)),
+            pltpu.SemaphoreType.REGULAR,
         ],
         compiler_params=pltpu.CompilerParams(
             collective_id=0, has_side_effects=True, vmem_limit_bytes=ROOM

time: 104 us -> 102 us (0.981)
  Pallas kernels: 103 us -> 101 us
    pallas_call x1, Pallas kernels: 58.6 us -> 56.7 us  [local(): pl.pallas_call(first_kernel, out_shape=(jax.ShapeDtypeStruct((19, CX, NY,...]
where the time goes in v4:
time: 102 us
  Pallas kernels  101 us (99%)
    pallas_call x1, Pallas kernels, local(): pl.pallas_call(first_kernel, out_shape=(jax.ShapeDtypeStruct((19, CX, NY,...  56.7 us
    pallas_call x1, Pallas kernels, local(): pl.pallas_call(second_kernel, out_shape=(jax.ShapeDtypeStruct((19, CX, NY...  44.3 us

profile of v4, /device:TPU:7, one launch (start us, length us, event | category | flops | bytes accessed | tf_op | source)
XLA Modules:
  0.0 101.7 jit_solution(10644276613045930283)
XLA Ops:
  0.6 56.7 %shard_map.77 = (f32[19,4,16,128]{3,2,1,0:T(8,128)}, f32[256,256]{1,0:T(8,128)}, f32[1152,256]{1,0:T(8,128)}, f32[4,8,128]{2,1,0:T(8,128)}) custom-call(f32[19,4,16,128]{3,2,1,0:T(8,128)} %pop_hbm.1, s32[4,16,128]{2,1,0:T(8,128)} %kind_hbm.1, s32[3]{0:T(128)} %phase_hbm.1, s32[4]{0:T(128)} %order_hbm.1, s32[384]{0:T(512)} %table_hbm.1, f32[1152,252]{1,0:T(8,128)} %modes_hbm.3), custom_call_target="tpu_custom_call" | custom-call | tf_op jit(solution)/shard_map/pallas_call | solution.py:826
  57.3 44.3 %shard_map.78 = (f32[19,4,16,128]{3,2,1,0:T(8,128)}, f32[1152,256]{1,0:T(8,128)}) custom-call(f32[1152,252]{1,0:T(8,128)} %modes_hbm.3, f32[19,4,16,128]{3,2,1,0:T(8,128)} %get-tuple-element.6.field, f32[256,256]{1,0:T(8,128)} %get-tuple-element.7.gram_hbm, f32[1152,256]{1,0:T(8,128)} %get-tuple-element.8.q_hbm, f32[4,8,128]{2,1,0:T(8,128)} %get-tuple-element.9.small_hbm), custom_call_target="tpu_custom_call" | custom-call | tf_op jit(solution)/shard_map/pallas_call | solution.py:891

commit v5 on v4

--- a/solution.py
+++ b/solution.py
@@ -50,7 +50,6 @@
 ROWS_DEV = 1152
 ROWS_ALL = 128 * ROWS_DEV
 SCALE = math.sqrt(ROWS_ALL)
-NEWTON = 2
 ROOM = 60 * 1024 * 1024
 LINE_FAR = [8, 7, 9, 6, 10, 5, 11, 4, 12, 3, 13, 2, 14, 1, 15]
 PLANE_FAR = [4, 5, 3, 6, 2, 7, 1]
@@ -67,23 +66,36 @@
     )
 
 
+def quick(a, b, dims):
+    return lax.dot_general(
+        a.astype(jnp.bfloat16),
+        b.astype(jnp.bfloat16),
+        (dims, ((), ())),
+        preferred_element_type=jnp.float32,
+    )
+
+
 def inflow_value(i):
     along = DIRS[i][0] * INLET
     return WEIGHTS[i] * (1.0 + 3.0 * along + 4.5 * along * along - 1.5 * INLET * INLET)
 
 
-def moments(f):
+def sums(f):
     density = f[0]
     for i in range(1, 19):
         density = density + f[i]
-    inverse = 1.0 / density
-    speeds = []
+    totals = []
     for axis in range(3):
         plus = [f[i] for i in range(19) if DIRS[i][axis] == 1]
         minus = [f[i] for i in range(19) if DIRS[i][axis] == -1]
-        total = functools.reduce(lambda a, b: a + b, [a - b for a, b in zip(plus, minus)])
-        speeds.append(total * inverse)
-    return density, speeds
+        totals.append(functools.reduce(lambda a, b: a + b, [a - b for a, b in zip(plus, minus)]))
+    return density, totals
+
+
+def moments(f):
+    density, totals = sums(f)
+    inverse = 1.0 / density
+    return density, [total * inverse for total in totals]
 
 
 def collide(f, kind):
@@ -213,17 +225,18 @@
     rest,
     speeds,
     samples,
-    early,
+    parts,
+    across,
+    ends,
     final,
     picks,
+    picks_next,
+    rows_next,
     landed_a,
-    landed_c,
     landed_b,
     ready_a,
-    ready_c,
     ready_b,
     got_a,
-    got_c,
     got_b,
     pack,
     slot_a,
@@ -234,8 +247,6 @@
     square,
     scaled,
     inverse,
-    snaps,
-    tails,
     cross_own,
     cross_a,
     cross_mid,
@@ -258,7 +269,7 @@
     has_east = jnp.logical_and(channel, position < 383)
     west_id = ((position - 1) // 128, (position + 127) % 128)
     east_id = ((position + 1) // 128, (position + 1) % 128)
-    ROUTE_A, ROUTE_C, ROUTE_B, LINE_A, LINE_C, LINE_B, GRAM_A, GRAM_B, GRAM_C, GRAM_D, CROSS_A, CROSS_B = range(12)
+    ROUTE_A, ROUTE_B, LINE_A, LINE_B, GRAM_A, GRAM_B, GRAM_C, GRAM_D, CROSS_A, CROSS_B = range(10)
     odd = slab % 2
 
     barrier = pltpu.get_barrier_semaphore()
@@ -305,6 +316,7 @@
         loads[5].start()
         loads[4].start()
         loads[3].start()
+        loads[2].start()
 
     def line_peer(d):
         return (group, ((zpos + d) % NLINE) * NPLANE + ppos)
@@ -422,13 +434,56 @@
         keep_speeds(u, kind, x)
         keep_post(post, x, slot + 1)
 
-    def last_plane(slot, x):
+    def keep_parts(f, kind, x):
+        density, totals = sums(f)
+        parts[x, 0] = jnp.where(kind == 1, 1.0, density)
+        for c in range(3):
+            parts[x, c + 1] = jnp.where(kind == 1, 0.0, totals[c])
+
+    def last_plane(slot, x, keep):
         kind = kind_ref[x]
         f = streamed(slot, x)
-        _, u = moments(f)
-        keep_speeds(u, kind, x)
+        if keep:
+            keep_parts(f, kind, x)
         for i in range(19):
             field[i, x] = jnp.where(kind == 1, pop[i, x], f[i])
+
+    def edge_parts(slot, x):
+        f = [None] * 19
+        for n, i in enumerate(REST):
+            if i == 0:
+                f[0] = rest[slot, x, 0]
+                continue
+            source = shifted(rest[slot, x, n], i)
+            f[i] = jnp.where(source >= 0.5 * BIG, rest[slot, x, REST.index(OPP[i])], source)
+        for n, i in enumerate(EAST):
+            back = west[slot, x + 1, WEST.index(OPP[i])]
+            if x == 0:
+                f[i] = jnp.where(shifted(east[slot - 1, 0, n], i) >= 0.5 * BIG, back, 0.0)
+            else:
+                source = shifted(east[slot, x, n], i)
+                f[i] = jnp.where(source >= 0.5 * BIG, back, source)
+        for n, i in enumerate(WEST):
+            back = east[slot, x + 1, EAST.index(OPP[i])]
+            if x == CX - 1:
+                f[i] = jnp.where(shifted(west[slot - 1, CX + 1, n], i) >= 0.5 * BIG, back, 0.0)
+            else:
+                source = shifted(west[slot, x + 2, n], i)
+                f[i] = jnp.where(source >= 0.5 * BIG, back, source)
+        keep_parts(f, kind_ref[x], x)
+
+    def out_parts(planes, dirs, wall):
+        total = [jnp.zeros((NY, NZ), jnp.float32)] * 4
+        for n, i in enumerate(dirs):
+            source = planes[n]
+            value = shifted(jnp.where(source >= 0.5 * BIG, 0.0, source), i)
+            total[0] = total[0] + value
+            for axis in range(3):
+                if DIRS[i][axis] == 1:
+                    total[axis + 1] = total[axis + 1] + value
+                elif DIRS[i][axis] == -1:
+                    total[axis + 1] = total[axis + 1] - value
+        return [jnp.where(wall, 0.0, value) for value in total]
 
     def pair(fn):
         def body(n, c):
@@ -450,7 +505,8 @@
         for d in FAR_ALL:
             hello((3, zpos * NPLANE + (ppos + d) % NPLANE))
 
-        samples[...] = jnp.zeros((STEPS, 4, NZ), jnp.float32)
+        samples[...] = jnp.zeros((2, 4, NZ), jnp.float32)
+        ends[...] = jnp.zeros((3, 4, NZ), jnp.float32)
 
         @pl.when(position == 0)
         def _():
@@ -494,7 +550,7 @@
             for d in FAR_ALL:
                 push(source, target.at[group * NPLANE + ppos], (3, zpos * NPLANE + (ppos + d) % NPLANE), n)
 
-        def one_step(slot, c):
+        def one_step(slot, c, sampled=True):
             pair(lambda n: middle_plane(slot, 1 + n))
 
             def one_side(side):
@@ -503,23 +559,38 @@
                 send_side(slot + 1, side)
 
             sides(one_side)
-            sample(slot)
+            if sampled:
+                sample(slot)
             return c
 
         lax.fori_loop(0, 2, one_step, 0)
         pl.semaphore_wait(go_sem, 8)
         to_analysis(samples.at[0:2], landed_a, ROUTE_A)
-        one_step(2, 0)
-        to_analysis(samples.at[2], landed_c, ROUTE_C)
-        pair(lambda n: last_plane(STEPS - 1, 1 + n))
+        one_step(2, 0, sampled=False)
+        last = STEPS - 1
+        edge_parts(last, 0)
+        edge_parts(last, CX - 1)
+        to_east = out_parts([east[last, CX, n] for n in range(5)], EAST, west[last - 1, CX + 1, 0] >= 0.5 * BIG)
+        to_west = out_parts([west[last, 1, n] for n in range(5)], WEST, east[last - 1, 0, 0] >= 0.5 * BIG)
+        for c in range(4):
+            across[c] = jnp.where(phase[0] == 0, to_east[c], jnp.where(phase[0] == CX - 1, to_west[c], 0.0))
+        pair(lambda n: last_plane(last, 1 + n, True))
+        lane11 = lax.broadcasted_iota(jnp.int32, (11, NY, NZ), 2)
+        row11 = lax.broadcasted_iota(jnp.int32, (11, NY, NZ), 1)
+        stack = [speeds[phase[0]].reshape(3 * NY, NZ), parts[phase[0]].reshape(4 * NY, NZ)]
+        stack = jnp.concatenate(stack + [across[...].reshape(4 * NY, NZ)], axis=0)
+        along = mm(stack, pick_z, ((1,), (0,))).reshape(11, NY, NZ)
+        chosen = jnp.sum(jnp.where(row11 == phase[1] + SUB * (lane11 // 32), along, 0.0), axis=1)
+        ends[0, 0:3] = chosen[0:3]
+        ends[1] = chosen[3:7]
+        ends[2] = chosen[7:11]
+        to_analysis(ends, landed_b, ROUTE_B)
 
         def last_side(side):
-            take_side(STEPS - 1, side)
-            last_plane(STEPS - 1, 3 * side)
+            take_side(last, side)
+            last_plane(last, 3 * side, False)
 
         sides(last_side)
-        sample(STEPS - 1)
-        to_analysis(samples.at[3], landed_b, ROUTE_B)
         stores[0].start()
 
         def sent(slot, c):
@@ -537,7 +608,6 @@
 
         lax.fori_loop(0, STEPS, sent, 0)
         left_here(landed_a.at[0:8], ROUTE_A)
-        left_here(landed_c.at[0:8], ROUTE_C)
         left_here(landed_b.at[0:8], ROUTE_B)
         stores[0].wait()
 
@@ -570,25 +640,47 @@
             )
 
         loads[3].wait()
+        loads[2].wait()
+
+        def shift(n, c):
+            home = (n // NPLANE) * 128 + zpos * NPLANE + n % NPLANE
+            there = home + jnp.where(phase[0] == 0, 1, -1)
+            inside = jnp.logical_and(there >= 0, there < 384)
+            used = jnp.logical_and(inside, jnp.logical_or(phase[0] == 0, phase[0] == CX - 1))
+            rows_next[n] = jnp.where(used, table[jnp.minimum(jnp.maximum(there, 0), 383)], -1)
+            return c
+
+        lax.fori_loop(0, 24, shift, 0)
 
         def pick(n, c):
             found = jnp.int32(-1)
+            found_next = jnp.int32(-1)
             wanted = 24 * (n // 3) + 3 * ppos + n % 3
             for g in range(3):
                 for p in range(NPLANE):
                     row = table[g * 128 + zpos * NPLANE + p]
                     found = jnp.where(row == wanted, g * NPLANE + p, found)
+                    row_next = rows_next[g * NPLANE + p]
+                    found_next = jnp.where(row_next == wanted, g * NPLANE + p, found_next)
             picks[n] = found
+            picks_next[n] = found_next
             return c
 
         lax.fori_loop(0, 48, pick, 0)
 
-        def forward(landed, ready, got, from_sem, to_sem):
+        def forward(landed, ready, got, from_sem, to_sem, split=False):
             arrived(landed, from_sem)
 
             def place(n, c):
                 source = picks[n]
-                ready[n] = jnp.where(source >= 0, landed[jnp.maximum(source, 0)], 0.0)
+                if split:
+                    other = picks_next[n]
+                    mine = jnp.maximum(source, 0)
+                    ready[n, 0] = jnp.where(source >= 0, landed[mine, 0], 0.0)
+                    own = jnp.where(source >= 0, landed[mine, 1], 0.0)
+                    ready[n, 1] = own + jnp.where(other >= 0, landed[jnp.maximum(other, 0), 2], 0.0)
+                else:
+                    ready[n] = jnp.where(source >= 0, landed[jnp.maximum(source, 0)], 0.0)
                 return c
 
             lax.fori_loop(0, 48, place, 0)
@@ -609,58 +701,30 @@
         arrived(column.at[0:15], GRAM_C)
         gram[ppos] = column[...]
         to_plane(column, gram.at[ppos], GRAM_D)
-        forward(landed_c, ready_c, got_c, ROUTE_C, LINE_C)
+        forward(landed_b, ready_b, got_b, ROUTE_B, LINE_B, split=True)
         arrived(gram.at[0:7], GRAM_D)
-        forward(landed_b, ready_b, got_b, ROUTE_B, LINE_B)
         for p in range(NPLANE):
             for z in range(NLINE):
                 down, across = 32 * p + 4 * (z // 2), 128 * (z % 2)
                 square[down : down + 4, across : across + 128] = gram[p, z]
         stores[1].start()
 
-        arrived(got_a.at[0:15], LINE_A)
-        arrived(got_c.at[0:15], LINE_C)
-        sum_a = jnp.sum(got_a[...], axis=0)
-        sum_c = jnp.sum(got_c[...], axis=0)
-        early[...] = jnp.zeros((3, 16, NZ), jnp.float32)
-        for t in range(3):
-            early[t, 0:4] = sum_a[t, 0]
-            early[t, 4:8] = sum_a[t, 1]
-            early[t, 8:12] = sum_c[t]
-        where_to = lax.broadcasted_iota(jnp.int32, (16, NZ), 1)
-        where_from = lax.broadcasted_iota(jnp.int32, (16, NZ), 0)
-        for t in range(3):
-            for c in range(3):
-                n = 3 * t + c
-                put = jnp.logical_and(where_from % 4 == c, where_to == 124 + where_from // 4)
-                put = jnp.logical_and(put, where_from < 12).astype(jnp.float32)
-                block = pl.ds(128 * n, 128)
-                tails[block, :] = mm(early[t], put, ((0,), (0,)))
-        snaps[...] = jnp.zeros((8, ROWS_DEV), jnp.float32)
-        for t in range(3):
-            for c in range(3):
-                n = 3 * t + c
-                for s in range(3):
-                    snaps[s : s + 1, 128 * n : 128 * n + 128] = early[t, 4 * s + c : 4 * s + c + 1]
-
         row, col, eye = square_iota()
         matrix, rs_row, _ = unit_diagonal(square[...])
         scaled[...] = matrix
-        inverse[...] = eye - lower_half(matrix - eye, row, col)
-
-        def newton(n, size):
-            here = inverse[...]
-            error = mm(mm(here, scaled[...], ((1,), (0,))), here, ((1,), (1,))) - eye
-            inverse[...] = here - mm(lower_half(error, row, col), here, ((1,), (0,)))
-            return jnp.sum(jnp.sum(error * error, axis=0, keepdims=True), axis=1, keepdims=True)
-
-        size = lax.fori_loop(0, NEWTON, newton, jnp.ones((1, 1), jnp.float32))
+        lower = lower_half(matrix - eye, row, col)
+        upper = (matrix - eye) - lower
+        mixed = quick(lower, matrix - eye, ((1,), (0,)))
+        second = lower_half(quick(mixed - upper, upper, ((1,), (0,))) - mixed, row, col)
+        inverse[...] = eye - lower - second + quick(second, lower, ((1,), (0,)))
+        here = inverse[...]
+        error = mm(mm(here, scaled[...], ((1,), (0,))), here, ((1,), (1,))) - eye
+        inverse[...] = here - quick(lower_half(error, row, col), here, ((1,), (0,)))
+        size = jnp.sum(jnp.sum(error * error, axis=0, keepdims=True), axis=1, keepdims=True)
         good = jnp.broadcast_to(size < 1e-6, (RANK, RANK))
         factor = jnp.where(good, inverse[...], eye) * rs_row
         inverse[...] = factor * SCALE
-        projected = mm(modes[...], inverse[:, 0:MODES], ((1,), (1,)))
-        q[:, 0:128] = projected[:, 0:128]
-        q[:, 128:RANK] = projected[:, 128:RANK] + tails[...]
+        q[...] = mm(modes[...], inverse[:, 0:MODES], ((1,), (1,)))
         stores[2].start()
         loads[4].wait()
         small[...] = jnp.zeros((4, 8, NZ), jnp.float32)
@@ -668,30 +732,38 @@
         for k in range(4):
             small[0, k + 1 : k + 2] = jnp.full((1, NZ), 1.0, jnp.float32) * order[k].astype(jnp.float32)
 
-        product = mm(snaps[...], q[...], ((1,), (0,)))
-        cross_own[0:3] = product[0:3, 0:128]
-        cross_own[4:7] = product[0:3, 128:RANK]
-
+        arrived(got_a.at[0:15], LINE_A)
+        final[...] = jnp.zeros((NZ, NZ), jnp.float32)
+        sum_a = jnp.sum(got_a[...], axis=0)
+        for t in range(3):
+            for s in range(2):
+                final[16 * s + 4 * t : 16 * s + 4 * t + 4] = sum_a[t, s]
         arrived(got_b.at[0:15], LINE_B)
         sum_b = jnp.sum(got_b[...], axis=0)
-        final[...] = jnp.zeros((NZ, NZ), jnp.float32)
         for t in range(3):
-            final[4 * t : 4 * t + 4] = sum_b[t]
+            final[32 + 4 * t : 36 + 4 * t] = sum_b[t, 0]
+            final[48 + 4 * t : 51 + 4 * t] = sum_b[t, 1, 1:4] / sum_b[t, 1, 0:1]
         tall = final[...].T
         lane = lax.broadcasted_iota(jnp.int32, (NZ, NZ), 1)
-        low_sum = jnp.zeros((8, NZ), jnp.float32)
-        high_sum = jnp.zeros((8, NZ), jnp.float32)
-        for t in range(3):
-            for c in range(3):
-                n = 3 * t + c
-                block = pl.ds(128 * n, 128)
-                wide = jnp.broadcast_to(tall[:, 4 * t + c : 4 * t + c + 1], (NZ, NZ))
-                high = jnp.where(lane == NZ - 1, wide, q[block, 128:RANK])
-                q[block, 128:RANK] = high
-                low_sum = low_sum + jnp.sum((wide * q[block, 0:128]).reshape(16, 8, NZ), axis=0)
-                high_sum = high_sum + jnp.sum((wide * high).reshape(16, 8, NZ), axis=0)
-        cross_own[3:4] = jnp.sum(low_sum, axis=0, keepdims=True)
-        cross_own[7:8] = jnp.sum(high_sum, axis=0, keepdims=True)
+        low_sum = [jnp.zeros((8, NZ), jnp.float32) for _ in range(STEPS)]
+        high_sum = [jnp.zeros((8, NZ), jnp.float32) for _ in range(STEPS)]
+        for n in range(9):
+            block = pl.ds(128 * n, 128)
+            spot = 4 * (n // 3) + n % 3
+            wide = []
+            for s in range(STEPS):
+                wide.append(jnp.broadcast_to(tall[:, 16 * s + spot : 16 * s + spot + 1], (NZ, NZ)))
+            low = q[block, 0:128]
+            high = q[block, 128:RANK]
+            for s in range(STEPS):
+                high = jnp.where(lane == 124 + s, wide[s], high)
+            q[block, 128:RANK] = high
+            for s in range(STEPS):
+                low_sum[s] = low_sum[s] + jnp.sum((wide[s] * low).reshape(16, 8, NZ), axis=0)
+                high_sum[s] = high_sum[s] + jnp.sum((wide[s] * high).reshape(16, 8, NZ), axis=0)
+        for s in range(STEPS):
+            cross_own[s : s + 1] = jnp.sum(low_sum[s], axis=0, keepdims=True)
+            cross_own[s + 4 : s + 5] = jnp.sum(high_sum[s], axis=0, keepdims=True)
 
         cross_a[zpos] = cross_own[...]
         to_line(cross_own, cross_a.at[zpos], CROSS_A)
@@ -714,7 +786,6 @@
         left_here(column.at[0:15], GRAM_C)
         left_here(gram.at[0:7], GRAM_D)
         left_here(got_a.at[0:15], LINE_A)
-        left_here(got_c.at[0:15], LINE_C)
         left_here(got_b.at[0:15], LINE_B)
         left_here(cross_a.at[0:15], CROSS_A)
         left_here(cross_b.at[0:7], CROSS_B)
@@ -848,19 +919,20 @@
             buffer(STEPS, CX + 2, 5, NY, NZ),
             buffer(STEPS, CX, 9, NY, NZ),
             buffer(CX, 3, NY, NZ),
-            buffer(STEPS, 4, NZ),
-            buffer(3, 16, NZ),
+            buffer(2, 4, NZ),
+            buffer(CX, 4, NY, NZ),
+            buffer(4, NY, NZ),
+            buffer(3, 4, NZ),
             buffer(NZ, NZ),
             pltpu.SMEM((48,), jnp.int32),
+            pltpu.SMEM((48,), jnp.int32),
+            pltpu.SMEM((24,), jnp.int32),
             buffer(24, 2, 4, NZ),
-            buffer(24, 4, NZ),
-            buffer(24, 4, NZ),
+            buffer(24, 3, 4, NZ),
             buffer(48, 2, 4, NZ),
-            buffer(48, 4, NZ),
-            buffer(48, 4, NZ),
+            buffer(48, 2, 4, NZ),
             buffer(NLINE, 3, 2, 4, NZ),
-            buffer(NLINE, 3, 4, NZ),
-            buffer(NLINE, 3, 4, NZ),
+            buffer(NLINE, 3, 2, 4, NZ),
             buffer(NPLANE, NLINE, 4, NZ),
             buffer(NPLANE, NLINE, 4, NZ),
             buffer(NLINE, 4, NZ),
@@ -870,8 +942,6 @@
             buffer(RANK, RANK),
             buffer(RANK, RANK),
             buffer(RANK, RANK),
-            buffer(8, ROWS_DEV),
-            buffer(ROWS_DEV, 128),
             buffer(8, NZ),
             buffer(NLINE, 8, NZ),
             buffer(8, NZ),
@@ -880,8 +950,8 @@
             dma((5,)),
             dma((STEPS, 2)),
             dma((STEPS, 2)),
-            dma((12,)),
-            dma((12,)),
+            dma((10,)),
+            dma((10,)),
             pltpu.SemaphoreType.REGULAR,
         ],
         compiler_params=pltpu.CompilerParams(

time: 102 us -> 97.2 us (0.953)
  Pallas kernels: 101 us -> 95.8 us
    pallas_call x1, Pallas kernels: 56.7 us -> 51.5 us  [local(): pl.pallas_call(first_kernel, out_shape=(jax.ShapeDtypeStruct((19, CX, NY,...]
where the time goes in v5:
time: 97.2 us; the launch traced here: 96.5 us
  Pallas kernels  95.8 us (99%)
    pallas_call x1, Pallas kernels, local(): pl.pallas_call(first_kernel, out_shape=(jax.ShapeDtypeStruct((19, CX, NY,...  51.5 us
    pallas_call x1, Pallas kernels, local(): pl.pallas_call(second_kernel, out_shape=(jax.ShapeDtypeStruct((19, CX, NY...  44.3 us

profile of v5, /device:TPU:7, one launch (start us, length us, event | category | flops | bytes accessed | tf_op | source)
XLA Modules:
  0.0 96.5 jit_solution(6988442674869410746)
XLA Ops:
  0.6 51.5 %shard_map.77 = (f32[19,4,16,128]{3,2,1,0:T(8,128)}, f32[256,256]{1,0:T(8,128)}, f32[1152,256]{1,0:T(8,128)}, f32[4,8,128]{2,1,0:T(8,128)}) custom-call(f32[19,4,16,128]{3,2,1,0:T(8,128)} %pop_hbm.1, s32[4,16,128]{2,1,0:T(8,128)} %kind_hbm.1, s32[3]{0:T(128)} %phase_hbm.1, s32[4]{0:T(128)} %order_hbm.1, s32[384]{0:T(512)} %table_hbm.1, f32[1152,252]{1,0:T(8,128)} %modes_hbm.3), custom_call_target="tpu_custom_call" | custom-call | tf_op jit(solution)/shard_map/pallas_call | solution.py:897
  52.1 44.3 %shard_map.78 = (f32[19,4,16,128]{3,2,1,0:T(8,128)}, f32[1152,256]{1,0:T(8,128)}) custom-call(f32[1152,252]{1,0:T(8,128)} %modes_hbm.3, f32[19,4,16,128]{3,2,1,0:T(8,128)} %get-tuple-element.6.field, f32[256,256]{1,0:T(8,128)} %get-tuple-element.7.gram_hbm, f32[1152,256]{1,0:T(8,128)} %get-tuple-element.8.q_hbm, f32[4,8,128]{2,1,0:T(8,128)} %get-tuple-element.9.small_hbm), custom_call_target="tpu_custom_call" | custom-call | tf_op jit(solution)/shard_map/pallas_call | solution.py:961

commit v6 on v5

--- a/solution.py
+++ b/solution.py
@@ -50,6 +50,7 @@
 ROWS_DEV = 1152
 ROWS_ALL = 128 * ROWS_DEV
 SCALE = math.sqrt(ROWS_ALL)
+PIECES = 1
 ROOM = 60 * 1024 * 1024
 LINE_FAR = [8, 7, 9, 6, 10, 5, 11, 4, 12, 3, 13, 2, 14, 1, 15]
 PLANE_FAR = [4, 5, 3, 6, 2, 7, 1]
@@ -440,11 +441,9 @@
         for c in range(3):
             parts[x, c + 1] = jnp.where(kind == 1, 0.0, totals[c])
 
-    def last_plane(slot, x, keep):
+    def last_plane(slot, x):
         kind = kind_ref[x]
         f = streamed(slot, x)
-        if keep:
-            keep_parts(f, kind, x)
         for i in range(19):
             field[i, x] = jnp.where(kind == 1, pop[i, x], f[i])
 
@@ -574,7 +573,8 @@
         to_west = out_parts([west[last, 1, n] for n in range(5)], WEST, east[last - 1, 0, 0] >= 0.5 * BIG)
         for c in range(4):
             across[c] = jnp.where(phase[0] == 0, to_east[c], jnp.where(phase[0] == CX - 1, to_west[c], 0.0))
-        pair(lambda n: last_plane(last, 1 + n, True))
+        for x in range(1, CX - 1):
+            keep_parts(streamed(last, x), kind_ref[x], x)
         lane11 = lax.broadcasted_iota(jnp.int32, (11, NY, NZ), 2)
         row11 = lax.broadcasted_iota(jnp.int32, (11, NY, NZ), 1)
         stack = [speeds[phase[0]].reshape(3 * NY, NZ), parts[phase[0]].reshape(4 * NY, NZ)]
@@ -586,9 +586,11 @@
         ends[2] = chosen[7:11]
         to_analysis(ends, landed_b, ROUTE_B)
 
+        pair(lambda n: last_plane(last, 1 + n))
+
         def last_side(side):
             take_side(last, side)
-            last_plane(last, 3 * side, False)
+            last_plane(last, 3 * side)
 
         sides(last_side)
         stores[0].start()
@@ -639,6 +641,34 @@
                 device_id_type=MESH,
             )
 
+        def forward(landed, ready, got, from_sem, to_sem, split=False):
+            arrived(landed, from_sem)
+
+            def place(n):
+                source = picks[n]
+                if split:
+                    other = picks_next[n]
+                    mine = jnp.maximum(source, 0)
+                    ready[n, 0] = jnp.where(source >= 0, landed[mine, 0], 0.0)
+                    own = jnp.where(source >= 0, landed[mine, 1], 0.0)
+                    ready[n, 1] = own + jnp.where(other >= 0, landed[jnp.maximum(other, 0), 2], 0.0)
+                else:
+                    ready[n] = jnp.where(source >= 0, landed[jnp.maximum(source, 0)], 0.0)
+
+            for d in LINE_FAR + [0]:
+                first = 3 * ((zpos + d) % NLINE)
+                for t in range(3):
+                    place(first + t)
+                if d:
+                    push(ready.at[pl.ds(first, 3)], got.at[zpos], line_peer(d), to_sem)
+                else:
+                    got[zpos] = ready[pl.ds(first, 3)]
+
+        arrived(slot_a.at[0:7], GRAM_A)
+        rows_a[...] = jnp.sum(slot_a[...], axis=0)
+        slot_b[zpos] = rows_a[zpos]
+        for d in LINE_FAR:
+            push(rows_a.at[(zpos + d) % NLINE], slot_b.at[zpos], line_peer(d), GRAM_B)
         loads[3].wait()
         loads[2].wait()
 
@@ -668,31 +698,6 @@
 
         lax.fori_loop(0, 48, pick, 0)
 
-        def forward(landed, ready, got, from_sem, to_sem, split=False):
-            arrived(landed, from_sem)
-
-            def place(n, c):
-                source = picks[n]
-                if split:
-                    other = picks_next[n]
-                    mine = jnp.maximum(source, 0)
-                    ready[n, 0] = jnp.where(source >= 0, landed[mine, 0], 0.0)
-                    own = jnp.where(source >= 0, landed[mine, 1], 0.0)
-                    ready[n, 1] = own + jnp.where(other >= 0, landed[jnp.maximum(other, 0), 2], 0.0)
-                else:
-                    ready[n] = jnp.where(source >= 0, landed[jnp.maximum(source, 0)], 0.0)
-                return c
-
-            lax.fori_loop(0, 48, place, 0)
-            got[zpos] = ready[pl.ds(3 * zpos, 3)]
-            for d in LINE_FAR:
-                push(ready.at[pl.ds(3 * ((zpos + d) % NLINE), 3)], got.at[zpos], line_peer(d), to_sem)
-
-        arrived(slot_a.at[0:7], GRAM_A)
-        rows_a[...] = jnp.sum(slot_a[...], axis=0)
-        slot_b[zpos] = rows_a[zpos]
-        for d in LINE_FAR:
-            push(rows_a.at[(zpos + d) % NLINE], slot_b.at[zpos], line_peer(d), GRAM_B)
         arrived(slot_b.at[0:15], GRAM_B)
         rows_b[...] = jnp.sum(slot_b[...], axis=0)
         column[zpos] = rows_b[...]
@@ -794,7 +799,7 @@
 
 
 def second_kernel(
-    modes_hbm, field, gram_hbm, q_hbm, small_hbm, lattice, basis, passing, q, small, ends, blank, modes, gram, left, inverse, pivots, sem
+    modes_hbm, field, gram_hbm, q_hbm, small_hbm, lattice, basis, passing, q, small, ends, modes, gram, left, inverse, pivots, sem
 ):
     group = lax.axis_index("group")
 
@@ -813,20 +818,23 @@
 
     @pl.when(group == 3)
     def _():
-        load_q = pltpu.make_async_copy(q_hbm, q, sem.at[0])
-        load_small = pltpu.make_async_copy(small_hbm, small, sem.at[1])
-        load_q.start()
+        load_small = pltpu.make_async_copy(small_hbm, small, sem.at[0])
         load_small.start()
-        blank[...] = jnp.zeros((CX, NY, NZ), jnp.float32)
-        clears = [pltpu.make_async_copy(blank, lattice.at[n], sem.at[4 + n]) for n in range(19)]
-        for clear in clears:
-            clear.start()
-        lane = lax.broadcasted_iota(jnp.int32, (ROWS_DEV, 128), 1)
+        blocks = [pl.ds(n * (ROWS_DEV // PIECES), ROWS_DEV // PIECES) for n in range(PIECES)]
+        loads = [
+            pltpu.make_async_copy(q_hbm.at[block], q.at[block], sem.at[4 + n]) for n, block in enumerate(blocks)
+        ]
+        for load in loads:
+            load.start()
+        passing[...] = jnp.zeros((19, CX, NY, NZ), jnp.float32)
+        clear = pltpu.make_async_copy(passing, lattice, sem.at[1])
         load_small.wait()
-        load_q.wait()
-
-        @pl.when(jnp.logical_not(small[0, 0, 0] < 1e-6))
+        good = small[0, 0, 0] < 1e-6
+
+        @pl.when(jnp.logical_not(good))
         def _():
+            for load in loads:
+                load.wait()
             load = pltpu.make_async_copy(modes_hbm, modes, sem.at[2])
             load.start()
             load_gram = pltpu.make_async_copy(gram_hbm, gram, sem.at[3])
@@ -873,17 +881,29 @@
             wide = lax.broadcasted_iota(jnp.int32, (ROWS_DEV, RANK), 1)
             q[...] = jnp.where(wide < MODES, whole, q[...])
 
-        first = pltpu.make_async_copy(q.at[:, 0:128], basis.at[:, 0:128], sem.at[0])
-        first.start()
         rows = jnp.concatenate([small[2, 0:4], small[3, 0:4]], axis=1)
         rows = jnp.concatenate([jnp.zeros((124, RANK), jnp.float32), rows], axis=0)
-        ends[...] = jnp.where(lane < 124, q[:, 128:RANK], mm(q[...], rows, ((1,), (1,))))
-        second = pltpu.make_async_copy(ends, basis.at[:, 128:RANK], sem.at[1])
-        second.start()
-        for clear in clears:
-            clear.wait()
-        first.wait()
-        second.wait()
+        lane = lax.broadcasted_iota(jnp.int32, (ROWS_DEV // PIECES, 128), 1)
+        clear.start()
+        stores = []
+        for n, block in enumerate(blocks):
+
+            @pl.when(good)
+            def _():
+                loads[n].wait()
+
+            stores.append(
+                pltpu.make_async_copy(q.at[block, 0:128], basis.at[block, 0:128], sem.at[4 + PIECES + n])
+            )
+            stores[-1].start()
+            ends[block] = jnp.where(lane < 124, q[block, 128:RANK], mm(q[block], rows, ((1,), (1,))))
+            stores.append(
+                pltpu.make_async_copy(ends.at[block], basis.at[block, 128:RANK], sem.at[4 + 2 * PIECES + n])
+            )
+            stores[-1].start()
+        clear.wait()
+        for store in stores:
+            store.wait()
 
 
 def local(populations, cell_kind, snapshot_order, sample_phase, slab_map, weighted_modes):
@@ -971,13 +991,12 @@
             buffer(ROWS_DEV, RANK),
             buffer(4, 8, NZ),
             buffer(ROWS_DEV, 128),
-            buffer(CX, NY, NZ),
             buffer(ROWS_DEV, MODES),
             buffer(RANK, RANK),
             buffer(RANK, RANK),
             buffer(RANK, RANK),
             buffer(RANK, 128),
-            dma((4 + 19,)),
+            dma((4 + 3 * PIECES,)),
         ],
         compiler_params=pltpu.CompilerParams(vmem_limit_bytes=ROOM),
     )(weighted_modes, field, gram, q, small)

time: 97.2 us -> 96.4 us (level)
  no operation moved by 1% of the time
where the time goes in v6:
time: 96.4 us; the launch traced here: 95.7 us
  Pallas kernels  95.1 us (99%)
    pallas_call x1, Pallas kernels, local(): pl.pallas_call(first_kernel, out_shape=(jax.ShapeDtypeStruct((19, CX, NY,...  51.1 us
    pallas_call x1, Pallas kernels, local(): pl.pallas_call(second_kernel, out_shape=(jax.ShapeDtypeStruct((19, CX, NY...  43.9 us

profile of v6, /device:TPU:7, one launch (start us, length us, event | category | flops | bytes accessed | tf_op | source)
XLA Modules:
  0.0 95.7 jit_solution(1351029176697497270)
XLA Ops:
  0.6 51.1 %shard_map.77 = (f32[19,4,16,128]{3,2,1,0:T(8,128)}, f32[256,256]{1,0:T(8,128)}, f32[1152,256]{1,0:T(8,128)}, f32[4,8,128]{2,1,0:T(8,128)}) custom-call(f32[19,4,16,128]{3,2,1,0:T(8,128)} %pop_hbm.1, s32[4,16,128]{2,1,0:T(8,128)} %kind_hbm.1, s32[3]{0:T(128)} %phase_hbm.1, s32[4]{0:T(128)} %order_hbm.1, s32[384]{0:T(512)} %table_hbm.1, f32[1152,252]{1,0:T(8,128)} %modes_hbm.3), custom_call_target="tpu_custom_call" | custom-call | tf_op jit(solution)/shard_map/pallas_call | solution.py:917
  51.8 43.9 %shard_map.78 = (f32[19,4,16,128]{3,2,1,0:T(8,128)}, f32[1152,256]{1,0:T(8,128)}) custom-call(f32[1152,252]{1,0:T(8,128)} %modes_hbm.3, f32[19,4,16,128]{3,2,1,0:T(8,128)} %get-tuple-element.6.field, f32[256,256]{1,0:T(8,128)} %get-tuple-element.7.gram_hbm, f32[1152,256]{1,0:T(8,128)} %get-tuple-element.8.q_hbm, f32[4,8,128]{2,1,0:T(8,128)} %get-tuple-element.9.small_hbm), custom_call_target="tpu_custom_call" | custom-call | tf_op jit(solution)/shard_map/pallas_call | solution.py:981

commit v7 on v6

--- a/solution.py
+++ b/solution.py
@@ -737,38 +737,43 @@
         for k in range(4):
             small[0, k + 1 : k + 2] = jnp.full((1, NZ), 1.0, jnp.float32) * order[k].astype(jnp.float32)
 
+        lane = lax.broadcasted_iota(jnp.int32, (NZ, NZ), 1)
+
+        def products(steps):
+            tall = final[...].T
+            low_sum = [jnp.zeros((8, NZ), jnp.float32) for _ in steps]
+            high_sum = [jnp.zeros((8, NZ), jnp.float32) for _ in steps]
+            for n in range(9):
+                block = pl.ds(128 * n, 128)
+                spot = 4 * (n // 3) + n % 3
+                wide = []
+                for s in steps:
+                    wide.append(jnp.broadcast_to(tall[:, 16 * s + spot : 16 * s + spot + 1], (NZ, NZ)))
+                low = q[block, 0:128]
+                high = q[block, 128:RANK]
+                for m, s in enumerate(steps):
+                    high = jnp.where(lane == 124 + s, wide[m], high)
+                q[block, 128:RANK] = high
+                for m in range(len(steps)):
+                    low_sum[m] = low_sum[m] + jnp.sum((wide[m] * low).reshape(16, 8, NZ), axis=0)
+                    high_sum[m] = high_sum[m] + jnp.sum((wide[m] * high).reshape(16, 8, NZ), axis=0)
+            for m, s in enumerate(steps):
+                cross_own[s : s + 1] = jnp.sum(low_sum[m], axis=0, keepdims=True)
+                cross_own[s + 4 : s + 5] = jnp.sum(high_sum[m], axis=0, keepdims=True)
+
         arrived(got_a.at[0:15], LINE_A)
         final[...] = jnp.zeros((NZ, NZ), jnp.float32)
         sum_a = jnp.sum(got_a[...], axis=0)
         for t in range(3):
             for s in range(2):
                 final[16 * s + 4 * t : 16 * s + 4 * t + 4] = sum_a[t, s]
+        products((0, 1))
         arrived(got_b.at[0:15], LINE_B)
         sum_b = jnp.sum(got_b[...], axis=0)
         for t in range(3):
             final[32 + 4 * t : 36 + 4 * t] = sum_b[t, 0]
             final[48 + 4 * t : 51 + 4 * t] = sum_b[t, 1, 1:4] / sum_b[t, 1, 0:1]
-        tall = final[...].T
-        lane = lax.broadcasted_iota(jnp.int32, (NZ, NZ), 1)
-        low_sum = [jnp.zeros((8, NZ), jnp.float32) for _ in range(STEPS)]
-        high_sum = [jnp.zeros((8, NZ), jnp.float32) for _ in range(STEPS)]
-        for n in range(9):
-            block = pl.ds(128 * n, 128)
-            spot = 4 * (n // 3) + n % 3
-            wide = []
-            for s in range(STEPS):
-                wide.append(jnp.broadcast_to(tall[:, 16 * s + spot : 16 * s + spot + 1], (NZ, NZ)))
-            low = q[block, 0:128]
-            high = q[block, 128:RANK]
-            for s in range(STEPS):
-                high = jnp.where(lane == 124 + s, wide[s], high)
-            q[block, 128:RANK] = high
-            for s in range(STEPS):
-                low_sum[s] = low_sum[s] + jnp.sum((wide[s] * low).reshape(16, 8, NZ), axis=0)
-                high_sum[s] = high_sum[s] + jnp.sum((wide[s] * high).reshape(16, 8, NZ), axis=0)
-        for s in range(STEPS):
-            cross_own[s : s + 1] = jnp.sum(low_sum[s], axis=0, keepdims=True)
-            cross_own[s + 4 : s + 5] = jnp.sum(high_sum[s], axis=0, keepdims=True)
+        products((2, 3))
 
         cross_a[zpos] = cross_own[...]
         to_line(cross_own, cross_a.at[zpos], CROSS_A)

time: 96.4 us -> 96 us (level)
  no operation moved by 1% of the time
where the time goes in v7:
time: 96 us; the launch traced here: 95.4 us
  Pallas kernels  94.7 us (99%)
    pallas_call x1, Pallas kernels, local(): pl.pallas_call(first_kernel, out_shape=(jax.ShapeDtypeStruct((19, CX, NY,...  50.8 us
    pallas_call x1, Pallas kernels, local(): pl.pallas_call(second_kernel, out_shape=(jax.ShapeDtypeStruct((19, CX, NY...  44 us

profile of v7, /device:TPU:7, one launch (start us, length us, event | category | flops | bytes accessed | tf_op | source)
XLA Modules:
  0.0 95.4 jit_solution(2296220477326143933)
XLA Ops:
  0.6 50.8 %shard_map.77 = (f32[19,4,16,128]{3,2,1,0:T(8,128)}, f32[256,256]{1,0:T(8,128)}, f32[1152,256]{1,0:T(8,128)}, f32[4,8,128]{2,1,0:T(8,128)}) custom-call(f32[19,4,16,128]{3,2,1,0:T(8,128)} %pop_hbm.1, s32[4,16,128]{2,1,0:T(8,128)} %kind_hbm.1, s32[3]{0:T(128)} %phase_hbm.1, s32[4]{0:T(128)} %order_hbm.1, s32[384]{0:T(512)} %table_hbm.1, f32[1152,252]{1,0:T(8,128)} %modes_hbm.3), custom_call_target="tpu_custom_call" | custom-call | tf_op jit(solution)/shard_map/pallas_call | solution.py:922
  51.4 44.0 %shard_map.78 = (f32[19,4,16,128]{3,2,1,0:T(8,128)}, f32[1152,256]{1,0:T(8,128)}) custom-call(f32[1152,252]{1,0:T(8,128)} %modes_hbm.3, f32[19,4,16,128]{3,2,1,0:T(8,128)} %get-tuple-element.6.field, f32[256,256]{1,0:T(8,128)} %get-tuple-element.7.gram_hbm, f32[1152,256]{1,0:T(8,128)} %get-tuple-element.8.q_hbm, f32[4,8,128]{2,1,0:T(8,128)} %get-tuple-element.9.small_hbm), custom_call_target="tpu_custom_call" | custom-call | tf_op jit(solution)/shard_map/pallas_call | solution.py:986
